TPU v7x, 32 devices: a whole 2x2x4 slice. The times are simulated.
32 devices in a mesh: grp: 4 (over z), shard: 8 (over y, x, core).
Axes of the slice: x: 2, y: 2, z: 4, core: 2. Of those that a mesh axis runs over, the one named last changes fastest.
Arguments:
- frames: bfloat16 [8192, 1024], P(('grp', 'shard')), may hold values from -6 to 6
- cotangent: bfloat16 [8192, 1024], P(('grp', 'shard')), may hold values from -6 to 6
- seg_start: int32 [32, 3], P(('grp', 'shard')), may hold values from 0 to 2047, as said below
- seg_length: int32 [32, 3], P(('grp', 'shard')), may hold values from 0 to 2044, as said below
- seg_step: int32 [32, 3], P(('grp', 'shard')), may hold values from 0 to 31, as said below
- time_table: float32 [32, 1024], replicated, may hold values from -6 to 6
- w_ada: bfloat16 [1024, 6144], P('shard', 'grp'), may hold values from -0.1875 to 0.1875
- b_ada: bfloat16 [6144], P('shard'), may hold values from -3 to 3
- w_qkv: bfloat16 [1024, 3072], P('shard', 'grp'), may hold values from -0.125 to 0.125
- b_qkv: bfloat16 [3072], P('shard'), may hold values from -0.29882812 to 0.29882812
- w_out: bfloat16 [1024, 1024], P('shard', 'grp'), may hold values from -1.5 to 1.5
- b_out: bfloat16 [1024], P('shard'), may hold values from -3 to 3
- w_up: bfloat16 [1024, 2048], P('shard', 'grp'), may hold values from -0.1875 to 0.1875
- b_up: bfloat16 [2048], P('shard'), may hold values from -3 to 3
- w_down: bfloat16 [2048, 1024], P('shard', 'grp'), may hold values from -0.125 to 0.125
- b_down: bfloat16 [1024], P('shard'), may hold values from -3 to 3
Outputs:
- output: bfloat16 [8192, 1024], P(('grp', 'shard'))
- grad_frames: float32 [8192, 1024], P(('grp', 'shard'))
- grad_time_table: float32 [32, 1024], P(None, 'shard')
- grad_w_ada: float32 [1024, 6144], P('shard', 'grp')
- grad_b_ada: float32 [6144], P('shard')
- grad_w_qkv: float32 [1024, 3072], P('shard', 'grp')
- grad_b_qkv: float32 [3072], P('shard')
- grad_w_out: float32 [1024, 1024], P('shard', 'grp')
- grad_b_out: float32 [1024], P('shard')
- grad_w_up: float32 [1024, 2048], P('shard', 'grp')
- grad_b_up: float32 [2048], P('shard')
- grad_w_down: float32 [2048, 1024], P('shard', 'grp')
- grad_b_down: float32 [1024], P('shard')
Inputs may be any that keep to these rules, and one draw needn't show every extreme that they name: `seg_start`: frame f lies at position f % 2048 of packed row f // 2048; row block b holds frames b * 256 to (b + 1) * 256 - 1. The 3 slots of block b list every segment that intersects it, by start position in its packed row; every frame lies in exactly one listed segment; slots of length 0 are empty and hold start 0. Segments stay inside their packed row, and in every packed row one segment starts in its first block and ends in its last, and the other segments lie inside the first or the last block. `seg_length`: A segment has the same start and length in every block that lists it. `seg_step`: A segment has the same timestep row in every block that lists it; empty slots hold 0.
All inputs are finite; a program needn't handle non-finite values.
Results may differ from a plain program's by a relative error of at most 0.014.
Values may be sent and summed in bfloat16 or wider, within the bound.
No kernel may reach another device: no remote copies, remote signals or barrier semaphores. Data moves between devices by JAX's collectives and lax.ppermute only.
A program may use at most 256 MiB of HBM per device.

v0:
```python
from functools import partial

import jax
import jax.numpy as jnp
from jax import lax
from jax.sharding import PartitionSpec as P

D = 1024
H = 16
HD = 64


eps_norm = 1e-06
top_precision = lax.Precision.HIGHEST


def normalize(tensor):
    centred = tensor - jnp.mean(tensor, axis=-1, keepdims=True)
    return centred * lax.rsqrt(jnp.mean(centred * centred, axis=-1, keepdims=True) + eps_norm)


def modulate(tensor, scale_vec, shift_vec):
    return normalize(tensor) * (1.0 + scale_vec) + shift_vec


def angles(positions):
    half_width = HD // 2
    inverse = 10000.0 ** (-jnp.arange(half_width, dtype=jnp.float32) / half_width)
    phase_grid = positions[:, None] * inverse[None, :]
    return (jnp.cos(phase_grid), jnp.sin(phase_grid))


def rotate(tensor, cosine_vals, sine_vals):
    row_total = tensor.shape[0]
    halves = tensor.reshape(row_total, H, 2, HD // 2)
    former = halves[:, :, 0]
    latter = halves[:, :, 1]
    cosine_part = cosine_vals[:, None, :]
    sine_part = sine_vals[:, None, :]
    turned = jnp.stack(
        (former * cosine_part - latter * sine_part, latter * cosine_part + former * sine_part),
        axis=2,
    )
    return turned.reshape(row_total, D)


def tile_width(row_total):
    for candidate in (512, 256, 128):
        return candidate
    return row_total


def head_view(tensor):
    return tensor.reshape(tensor.shape[0], H, HD)


def local(
    frames,
    cotangent,
    seg_start,
    seg_length,
    seg_step,
    time_table,
    w_ada,
    b_ada,
    w_qkv,
    b_qkv,
    w_out,
    b_out,
    w_up,
    b_up,
    w_down,
    b_down,
):
    frame_rows = frames.shape[0]
    positions = lax.axis_index("shard") * frame_rows + jnp.arange(frame_rows, dtype=jnp.int32)
    slot_start = seg_start[0]
    slot_end = slot_start + seg_length[0]
    member_mask = (positions[:, None] >= slot_start[None, :]) & (
        positions[:, None] < slot_end[None, :]
    )
    member = member_mask.astype(jnp.float32)
    seg_low = jnp.sum(jnp.where(member_mask, slot_start[None, :], 0), axis=1)
    seg_high = jnp.sum(jnp.where(member_mask, slot_end[None, :], 0), axis=1)
    cosine_vals, sine_vals = angles((positions - seg_low).astype(jnp.float32))
    columns = (
        lax.all_gather(w_ada, "grp", axis=1, tiled=True),
        lax.all_gather(w_qkv, "grp", axis=1, tiled=True),
        lax.all_gather(w_out, "grp", axis=1, tiled=True),
        lax.all_gather(w_up, "grp", axis=1, tiled=True),
        lax.all_gather(w_down, "grp", axis=1, tiled=True),
    )
    gathered = (
        lax.all_gather(columns[0], "shard", axis=0, tiled=True),
        lax.all_gather(columns[1], "shard", axis=0, tiled=True),
        lax.all_gather(columns[2], "shard", axis=0, tiled=True),
        lax.all_gather(columns[3], "shard", axis=0, tiled=True),
        lax.all_gather(columns[4], "shard", axis=0, tiled=True),
        lax.all_gather(b_ada, "shard", axis=0, tiled=True),
        lax.all_gather(b_qkv, "shard", axis=0, tiled=True),
        lax.all_gather(b_out, "shard", axis=0, tiled=True),
        lax.all_gather(b_up, "shard", axis=0, tiled=True),
        lax.all_gather(b_down, "shard", axis=0, tiled=True),
    )
    ada_full, qkv_full, out_full, up_full, down_full = (
        gathered[0],
        gathered[1],
        gathered[2],
        gathered[3],
        gathered[4],
    )
    ada_bias, qkv_bias, out_bias, up_bias, down_bias = [
        bias_row.astype(jnp.float32) for bias_row in gathered[5:]
    ]
    step_onehot = (
        seg_step[0][:, None] == jnp.arange(time_table.shape[0], dtype=jnp.int32)[None, :]
    ).astype(jnp.float32)
    time_rows = jnp.dot(step_onehot, time_table, precision=top_precision)
    activated = jax.nn.silu(time_rows).astype(jnp.bfloat16)
    modulation = jnp.dot(activated, ada_full, preferred_element_type=jnp.float32) + ada_bias
    frame_mod = jnp.dot(member, modulation, precision=top_precision)
    shift_attn, scale_attn, gate_attn, shift_ff, scale_ff, gate_ff = jnp.split(frame_mod, 6, axis=1)
    inputs = frames.astype(jnp.float32)
    hidden_attn = modulate(inputs, scale_attn, shift_attn).astype(jnp.bfloat16)
    projected = jnp.dot(hidden_attn, qkv_full, preferred_element_type=jnp.float32) + qkv_bias
    queries = rotate(projected[:, :D], cosine_vals, sine_vals).astype(jnp.bfloat16)
    keys_rot = rotate(projected[:, D : 2 * D], cosine_vals, sine_vals).astype(jnp.bfloat16)
    values = projected[:, 2 * D :].astype(jnp.bfloat16)
    query_heads = head_view(queries)
    key_heads = head_view(keys_rot)
    value_heads = head_view(values)
    zero_heads = jnp.zeros((frame_rows, H, HD), jnp.float32)
    key_piece = lax.all_gather(keys_rot, "shard", axis=0, tiled=True)
    value_piece = lax.all_gather(values, "shard", axis=0, tiled=True)
    piece_rows = key_piece.shape[0]
    tile_rows = tile_width(piece_rows)
    tiles = piece_rows // tile_rows

    def tile_step(partial_sums, tile_item):
        key_tile, value_tile, offset = tile_item
        key_pos = offset + jnp.arange(tile_rows, dtype=jnp.int32)
        inside = (key_pos[None, :] >= seg_low[:, None]) & (key_pos[None, :] < seg_high[:, None])
        scores = 0.125 * jnp.einsum(
            "rhd,khd->hrk", query_heads, head_view(key_tile), preferred_element_type=jnp.float32
        )
        expo = jnp.where(inside[None], jnp.exp(scores), 0.0)
        numerator, denominator = partial_sums
        numerator = numerator + jnp.einsum(
            "hrk,khd->rhd",
            expo.astype(jnp.bfloat16),
            head_view(value_tile),
            preferred_element_type=jnp.float32,
        )
        denominator = denominator + jnp.sum(expo, axis=2).T
        return ((numerator, denominator), None)

    tile_items = (
        key_piece.reshape(tiles, tile_rows, D),
        value_piece.reshape(tiles, tile_rows, D),
        jnp.arange(tiles, dtype=jnp.int32) * tile_rows,
    )
    numerator, denominator = lax.scan(
        tile_step, (zero_heads, jnp.zeros((frame_rows, H), jnp.float32)), tile_items
    )[0]
    mixed = numerator / denominator[:, :, None]
    mixed_low = mixed.reshape(frame_rows, D).astype(jnp.bfloat16)
    attn_branch = jnp.dot(mixed_low, out_full, preferred_element_type=jnp.float32) + out_bias
    after_attn = inputs + gate_attn * attn_branch
    hidden_ff = modulate(after_attn, scale_ff, shift_ff).astype(jnp.bfloat16)
    upward = jnp.dot(hidden_ff, up_full, preferred_element_type=jnp.float32) + up_bias
    activation = jax.nn.gelu(upward, approximate=True).astype(jnp.bfloat16)
    ff_branch = jnp.dot(activation, down_full, preferred_element_type=jnp.float32) + down_bias
    output = (after_attn + gate_ff * ff_branch).astype(jnp.bfloat16)
    columns_back = (
        lax.all_gather(w_ada, "grp", axis=1, tiled=True),
        lax.all_gather(w_qkv, "grp", axis=1, tiled=True),
        lax.all_gather(w_out, "grp", axis=1, tiled=True),
        lax.all_gather(w_up, "grp", axis=1, tiled=True),
        lax.all_gather(w_down, "grp", axis=1, tiled=True),
    )
    gathered_back = (
        lax.all_gather(columns_back[0], "shard", axis=0, tiled=True),
        lax.all_gather(columns_back[1], "shard", axis=0, tiled=True),
        lax.all_gather(columns_back[2], "shard", axis=0, tiled=True),
        lax.all_gather(columns_back[3], "shard", axis=0, tiled=True),
        lax.all_gather(columns_back[4], "shard", axis=0, tiled=True),
    )
    ada_back, qkv_back, out_back, up_back, down_back = (
        gathered_back[0],
        gathered_back[1],
        gathered_back[2],
        gathered_back[3],
        gathered_back[4],
    )
    grad_out = cotangent.astype(jnp.float32)
    d_branch = (gate_ff * grad_out).astype(jnp.bfloat16)
    d_gate_ff = grad_out * ff_branch
    g_down = jnp.dot(activation.T, d_branch, preferred_element_type=jnp.float32)
    gb_down = jnp.sum(d_branch.astype(jnp.float32), axis=0)
    d_activation = jnp.dot(d_branch, down_back.T, preferred_element_type=jnp.float32)
    gelu_pull = jax.vjp(partial(jax.nn.gelu, approximate=True), upward)[1]
    d_upward = gelu_pull(d_activation)[0].astype(jnp.bfloat16)
    g_up = jnp.dot(hidden_ff.T, d_upward, preferred_element_type=jnp.float32)
    gb_up = jnp.sum(d_upward.astype(jnp.float32), axis=0)
    d_hidden_ff = jnp.dot(d_upward, up_back.T, preferred_element_type=jnp.float32)
    ff_pull = jax.vjp(modulate, after_attn, scale_ff, shift_ff)[1]
    dx_ff, d_scale_ff, d_shift_ff = ff_pull(d_hidden_ff)
    d_after = grad_out + dx_ff
    d_attn = (gate_attn * d_after).astype(jnp.bfloat16)
    d_gate_attn = d_after * attn_branch
    g_out = jnp.dot(mixed_low.T, d_attn, preferred_element_type=jnp.float32)
    gb_out = jnp.sum(d_attn.astype(jnp.float32), axis=0)
    d_mixed = jnp.dot(d_attn, out_back.T, preferred_element_type=jnp.float32).astype(jnp.bfloat16)
    d_mixed_heads = head_view(d_mixed).astype(jnp.float32)
    delta = jnp.sum(d_mixed_heads * mixed, axis=2) / denominator
    d_numer = (d_mixed_heads / denominator[:, :, None]).astype(jnp.bfloat16).reshape(frame_rows, D)
    dnum_heads = head_view(d_numer)
    delta_heads = delta.T
    key_piece = lax.all_gather(keys_rot, "shard", axis=0, tiled=True)
    value_piece = lax.all_gather(values, "shard", axis=0, tiled=True)
    piece_rows = key_piece.shape[0]
    fold_tile_rows = tile_width(piece_rows)
    tiles = piece_rows // fold_tile_rows

    def tile_step(grad_sum, tile_item):
        key_tile, value_tile, offset = tile_item
        key_pos = offset + jnp.arange(fold_tile_rows, dtype=jnp.int32)
        inside = (key_pos[None, :] >= seg_low[:, None]) & (key_pos[None, :] < seg_high[:, None])
        scores = 0.125 * jnp.einsum(
            "rhd,khd->hrk", query_heads, head_view(key_tile), preferred_element_type=jnp.float32
        )
        expo = jnp.where(inside[None], jnp.exp(scores), 0.0)
        slope = jnp.einsum(
            "rhd,khd->hrk", dnum_heads, head_view(value_tile), preferred_element_type=jnp.float32
        )
        d_scores = (expo * (slope - delta_heads[:, :, None])).astype(jnp.bfloat16)
        grad_sum = grad_sum + 0.125 * jnp.einsum(
            "hrk,khd->rhd", d_scores, head_view(key_tile), preferred_element_type=jnp.float32
        )
        return (grad_sum, None)

    tile_items = (
        key_piece.reshape(tiles, fold_tile_rows, D),
        value_piece.reshape(tiles, fold_tile_rows, D),
        jnp.arange(tiles, dtype=jnp.int32) * fold_tile_rows,
    )
    d_query = lax.scan(tile_step, zero_heads, tile_items)[0]
    delta_all = lax.all_gather(delta, "shard", axis=0, tiled=True)

    def fold_key_grad(running, piece):
        query_piece, dnum_piece = piece
        piece_rows = query_piece.shape[0]
        tile_rows = tile_width(piece_rows)
        tiles = piece_rows // tile_rows

        def tile_step(grad_pair, tile_item):
            query_tile, dnum_tile, delta_tile, offset = tile_item
            query_pos = offset + jnp.arange(tile_rows, dtype=jnp.int32)
            inside = (query_pos[:, None] >= seg_low[None, :]) & (
                query_pos[:, None] < seg_high[None, :]
            )
            query_tile_heads = head_view(query_tile)
            dnum_tile_heads = head_view(dnum_tile)
            scores = 0.125 * jnp.einsum(
                "qhd,rhd->hqr", query_tile_heads, key_heads, preferred_element_type=jnp.float32
            )
            expo = jnp.where(inside[None], jnp.exp(scores), 0.0)
            slope = jnp.einsum(
                "qhd,rhd->hqr", dnum_tile_heads, value_heads, preferred_element_type=jnp.float32
            )
            d_scores = (expo * (slope - delta_tile.T[:, :, None])).astype(jnp.bfloat16)
            d_keys, d_values = grad_pair
            d_keys = d_keys + 0.125 * jnp.einsum(
                "hqr,qhd->rhd", d_scores, query_tile_heads, preferred_element_type=jnp.float32
            )
            d_values = d_values + jnp.einsum(
                "hqr,qhd->rhd",
                expo.astype(jnp.bfloat16),
                dnum_tile_heads,
                preferred_element_type=jnp.float32,
            )
            return ((d_keys, d_values), None)

        tile_items = (
            query_piece.reshape(tiles, tile_rows, D),
            dnum_piece.reshape(tiles, tile_rows, D),
            delta_all.reshape(tiles, tile_rows, H),
            jnp.arange(tiles, dtype=jnp.int32) * tile_rows,
        )
        return lax.scan(tile_step, running, tile_items)[0]

    d_keys, d_values = fold_key_grad(
        (zero_heads, zero_heads),
        (
            lax.all_gather(queries, "shard", axis=0, tiled=True),
            lax.all_gather(d_numer, "shard", axis=0, tiled=True),
        ),
    )
    grad_query = rotate(d_query.reshape(frame_rows, D), cosine_vals, -sine_vals)
    grad_key = rotate(d_keys.reshape(frame_rows, D), cosine_vals, -sine_vals)
    d_projected = jnp.concatenate(
        (grad_query, grad_key, d_values.reshape(frame_rows, D)), axis=1
    ).astype(jnp.bfloat16)
    g_qkv = jnp.dot(hidden_attn.T, d_projected, preferred_element_type=jnp.float32)
    gb_qkv = jnp.sum(d_projected.astype(jnp.float32), axis=0)
    d_hidden_attn = jnp.dot(d_projected, qkv_back.T, preferred_element_type=jnp.float32)
    attn_pull = jax.vjp(modulate, inputs, scale_attn, shift_attn)[1]
    dx_attn, d_scale_attn, d_shift_attn = attn_pull(d_hidden_attn)
    grad_frames = d_after + dx_attn
    d_frame_mod = jnp.concatenate(
        (d_shift_attn, d_scale_attn, d_gate_attn, d_shift_ff, d_scale_ff, d_gate_ff), axis=1
    )
    d_slot = jnp.dot(member.T, d_frame_mod, precision=top_precision)
    g_ada = jnp.dot(activated.astype(jnp.float32).T, d_slot, precision=top_precision)
    gb_ada = jnp.sum(d_slot, axis=0)
    d_activated = jnp.dot(
        d_slot, ada_back.T, precision=top_precision, preferred_element_type=jnp.float32
    )
    silu_pull = jax.vjp(jax.nn.silu, time_rows)[1]
    d_time_rows = silu_pull(d_activated)[0]
    g_table = jnp.dot(step_onehot.T, d_time_rows, precision=top_precision)
    group_sums = (
        lax.psum_scatter(g_ada, "shard", scatter_dimension=0, tiled=True),
        lax.psum_scatter(g_qkv, "shard", scatter_dimension=0, tiled=True),
        lax.psum_scatter(g_out, "shard", scatter_dimension=0, tiled=True),
        lax.psum_scatter(g_up, "shard", scatter_dimension=0, tiled=True),
        lax.psum_scatter(g_down, "shard", scatter_dimension=0, tiled=True),
        lax.psum_scatter(gb_ada, "shard", scatter_dimension=0, tiled=True),
        lax.psum_scatter(gb_qkv, "shard", scatter_dimension=0, tiled=True),
        lax.psum_scatter(gb_out, "shard", scatter_dimension=0, tiled=True),
        lax.psum_scatter(gb_up, "shard", scatter_dimension=0, tiled=True),
        lax.psum_scatter(gb_down, "shard", scatter_dimension=0, tiled=True),
        lax.psum_scatter(g_table, "shard", scatter_dimension=1, tiled=True),
    )
    wide_sums = (
        lax.psum_scatter(group_sums[0], "grp", scatter_dimension=1, tiled=True),
        lax.psum_scatter(group_sums[1], "grp", scatter_dimension=1, tiled=True),
        lax.psum_scatter(group_sums[2], "grp", scatter_dimension=1, tiled=True),
        lax.psum_scatter(group_sums[3], "grp", scatter_dimension=1, tiled=True),
        lax.psum_scatter(group_sums[4], "grp", scatter_dimension=1, tiled=True),
    )
    small_sums = lax.psum(
        (group_sums[5], group_sums[6], group_sums[7], group_sums[8], group_sums[9], group_sums[10]),
        "grp",
    )
    finals = tuple(wide_sums) + tuple(small_sums)
    return (
        output,
        grad_frames,
        finals[10],
        finals[0],
        finals[5],
        finals[1],
        finals[6],
        finals[2],
        finals[7],
        finals[3],
        finals[8],
        finals[4],
        finals[9],
    )


def solution(mesh):
    in_specs = (
        P(("grp", "shard"), None),
        P(("grp", "shard"), None),
        P(("grp", "shard"), None),
        P(("grp", "shard"), None),
        P(("grp", "shard"), None),
        P(),
        P("shard", "grp"),
        P("shard"),
        P("shard", "grp"),
        P("shard"),
        P("shard", "grp"),
        P("shard"),
        P("shard", "grp"),
        P("shard"),
        P("shard", "grp"),
        P("shard"),
    )
    out_specs = (
        P(("grp", "shard"), None),
        P(("grp", "shard"), None),
        P(None, "shard"),
        P("shard", "grp"),
        P("shard"),
        P("shard", "grp"),
        P("shard"),
        P("shard", "grp"),
        P("shard"),
        P("shard", "grp"),
        P("shard"),
        P("shard", "grp"),
        P("shard"),
    )
    return jax.shard_map(local, mesh=mesh, in_specs=in_specs, out_specs=out_specs, check_vma=False)
```

profile of v0, /device:TPU:0, one launch (start us, length us, event | category | flops | bytes accessed | tf_op | source)
XLA Modules:
  0.0 1127.1 jit_solution(16731711766397166424)
XLA Ops:
  8.0 41.5 %all-gather.16.cloned.1.call-done = bf16[128,6144]{1,0:T(8,128)(2,1)} async-done(((bf16[128,1536]{1,0:T(8,128)(2,1)}), bf16[128,6144]{1,0:T(8,128)(2,1)}) %all-gather.16.cloned.1.call-update) | async-done | bytes 1572880 | tf_op jit(solution)/shard_map/all_gather | solution.py:87
  49.5 18.6 %all_gather.75 = bf16[128,3072]{1,0:T(8,128)(2,1)} all-gather(bf16[128,768]{1,0:T(8,128)(2,1)} %param.30), channel_id=1, replica_groups=mesh['grp'=4,'shard'=8] {'grp'}, dimensions={1}, use_global_device_ids=true | all-gather | bytes 983040 | tf_op jit(solution)/shard_map/all_gather | solution.py:88
  68.9 9.1 all-gather
  89.6 32.9 %all-gather.18.cloned.1.call-done = bf16[1024,6144]{1,0:T(8,128)(2,1)} async-done(((bf16[128,6144]{1,0:T(8,128)(2,1)}), bf16[1024,6144]{1,0:T(8,128)(2,1)}) %all-gather.18.cloned.1.call-update) | async-done | bytes 12582928 | tf_op jit(solution)/shard_map/all_gather | solution.py:94
  134.4 35.5 %all-gather.20.cloned.1.call-done = bf16[1024,3072]{1,0:T(8,128)(2,1)} async-done(((bf16[128,3072]{1,0:T(8,128)(2,1)}), bf16[1024,3072]{1,0:T(8,128)(2,1)}) %all-gather.20.cloned.1.call-update) | async-done | bytes 6291472 | tf_op jit(solution)/shard_map/all_gather | solution.py:95
  181.9 14.6 %all_gather.80 = bf16[128,1024]{1,0:T(8,128)(2,1)} all-gather(bf16[128,256]{1,0:T(8,128)(2,1)S(1)} %copy-done.37), channel_id=1, replica_groups=mesh['grp'=4,'shard'=8] {'grp'}, dimensions={1}, use_global_device_ids=true | all-gather | bytes 327680 | tf_op jit(solution)/shard_map/all_gather | solution.py:89
  196.6 16.3 %all_gather.86 = bf16[256,1024]{1,0:T(8,128)(2,1)} all-gather(bf16[256,256]{1,0:T(8,128)(2,1)S(1)} %copy-done.36), channel_id=1, replica_groups=mesh['grp'=4,'shard'=8] {'grp'}, dimensions={1}, use_global_device_ids=true | all-gather | bytes 655360 | tf_op jit(solution)/shard_map/all_gather | solution.py:91
  213.0 16.9 %all_gather.83 = bf16[128,2048]{1,0:T(8,128)(2,1)} all-gather(bf16[128,512]{1,0:T(8,128)(2,1)} %param.34), channel_id=1, replica_groups=mesh['grp'=4,'shard'=8] {'grp'}, dimensions={1}, use_global_device_ids=true | all-gather | bytes 655360 | tf_op jit(solution)/shard_map/all_gather | solution.py:90
  256.3 11.3 %all-gather.34.cloned.1.call-start = ((), (), s32[]{:S(2)}) async-start(), calls=%async_computation.20 | async-start | bytes 4718592 | tf_op jit(solution)/shard_map/all_gather | solution.py:296
  286.7 54.8 %while.37 = (s32[]{:T(128)}, f32[256,16,64]{0,2,1:T(8,128)S(1)}, f32[256,16]{0,1:T(8,128)S(1)}, bf16[4,512,1024]{1,2,0:T(8,128)(2,1)}, s32[4]{0:T(128)S(1)}, /*i...) while((s32[]{:T(128)}, f32[256,16,64]{0,2,1:T(8,128)S(1)}, ...), condition=%wide.region_6.7_spmd.clone, body=%wide.region_4.6_spmd.clone.sunk | while | flops 550375936 | bytes 26155148 | solution.py:162
  402.3 62.8 %while.38 = (s32[]{:T(128)}, f32[256,16,64]{0,2,1:T(8,128)}, bf16[4,512,1024]{1,2,0:T(8,128)(2,1)}, s32[4]{0:T(128)S(1)}, s32[256]{0:T(256)S(1)}, /*index=5*/s32...) while((s32[]{:T(128)}, f32[256,16,64]{0,2,1:T(8,128)}, ...), condition=%wide.region_13.14_spmd.clone, body=%wide.region_12.13_spmd.clone.sunk | while | flops 816972288 | bytes 27547796 | solution.py:247
  465.1 10.1 all_gather.91
  481.8 98.6 %while.39 = (s32[]{:T(128)}, f32[256,16,64]{0,2,1:T(8,128)}, f32[256,16,64]{0,2,1:T(8,128)}, bf16[4,512,1024]{2,1,0:T(8,128)(2,1)}, s32[4]{0:T(128)S(1)}, /*inde...) while((s32[]{:T(128)}, f32[256,16,64]{0,2,1:T(8,128)}, ...), condition=%wide.region_15.16_spmd.clone, body=%wide.region_14.15_spmd.clone.sunk | while | flops 1092223488 | bytes 51943636 | solution.py:290
  604.6 13.5 %fusion.94 = f32[1024,6144]{1,0:T(8,128)} fusion(f32[3,6144]{1,0:T(4,128)S(1)} %get-tuple-element.514, f32[3,1024]{1,0:T(4,128)S(1)} %copy-done.34), kind=kOutput, calls=%fused_computation.167 | convolution fusion | flops 226507776 | bytes 25251840 | tf_op jit(solution)/shard_map/dot_general | solution.py:314
  618.1 12.7 %fusion.109 = f32[3,1024]{1,0:T(4,128)S(1)} fusion(f32[3,6144]{1,0:T(4,128)S(1)} %get-tuple-element.514, bf16[1024,6144]{1,0:T(8,128)(2,1)} %all-gather.18.cloned.1.call-done), kind=kOutput, calls=%fused_computation.180 | convolution fusion | flops 226492416 | bytes 12668928 | tf_op jit(solution)/shard_map/dot_general | solution.py:316
  633.1 13.2 %reduce-scatter.30.cloned.1.call-done = f32[256,1024]{1,0:T(8,128)} async-done(((f32[2048,1024]{1,0:T(8,128)}), f32[256,1024]{1,0:T(8,128)}) %reduce-scatter.30.cloned.1.call-update) | async-done | bytes 1048592 | tf_op jit(solution)/shard_map/reduce_scatter | solution.py:327
  646.4 96.1 %reduce-scatter.18.cloned.1.call-done = f32[128,3072]{1,0:T(8,128)} async-done(((f32[1024,3072]{1,0:T(8,128)}), f32[128,3072]{1,0:T(8,128)}) %reduce-scatter.18.cloned.1.call-update) | async-done | bytes 1572880 | tf_op jit(solution)/shard_map/reduce_scatter | solution.py:324
  742.5 160.8 %reduce-scatter.14.cloned.1.call-done = f32[128,6144]{1,0:T(8,128)} async-done(((f32[1024,6144]{1,0:T(8,128)}), f32[128,6144]{1,0:T(8,128)}) %reduce-scatter.14.cloned.1.call-update) | async-done | bytes 3145744 | tf_op jit(solution)/shard_map/reduce_scatter | solution.py:323
  907.0 23.7 %all-reduce.5 = (f32[6144]{0:T(1024)S(1)}, f32[3072]{0:T(1024)S(1)}, f32[1024]{0:T(1024)S(1)}, f32[2048]{0:T(1024)S(1)}, f32[1024]{0:T(1024)S(1)}) all-reduce(f32[6144]{0:T(1024)S(1)} %get-tuple-element.513, f32[3072]{0:T(1024)S(1)} %convert_reduce_fusion, ...), channel_id=5, replica_groups=mesh['grp'=4,'shard'=8] {'shard'}, use_global_device_ids=true, to_apply=%region_23.24.clone | all-reduce | flops 13312 | bytes 106496
  939.8 19.8 %all-reduce.6 = (f32[32,128]{1,0:T(8,128)}, f32[768]{0:T(1024)}, f32[384]{0:T(512)}, f32[128]{0:T(128)}, f32[256]{0:T(256)}, /*index=5*/f32[128]{0:T(128)}) all-reduce(f32[32,128]{1,0:T(8,128)} %reduce-scatter.12.cloned.1.call-done, f32[768]{0:T(1024)S(1)} %dynamic-slice.1, ...), channel_id=1, replica_groups=mesh['grp'=4,'shard'=8] {'grp'}, use_global_device_ids=true, to_apply=%region_19.20 | all-reduce | flops 5760 | bytes 46080 | tf_op jit(solution)/shard_map/psum | solution.py:342
  964.4 28.1 %reduce-scatter.28.cloned.1.call-done = f32[128,512]{1,0:T(8,128)} async-done(((f32[128,2048]{1,0:T(8,128)}), f32[128,512]{1,0:T(8,128)}) %reduce-scatter.28.cloned.1.call-update) | async-done | bytes 262160 | tf_op jit(solution)/shard_map/reduce_scatter | solution.py:339
  992.4 28.8 %reduce-scatter.32.cloned.1.call-done = f32[256,256]{1,0:T(8,128)} async-done(((f32[256,1024]{1,0:T(8,128)}), f32[256,256]{1,0:T(8,128)}) %reduce-scatter.32.cloned.1.call-update) | async-done | bytes 262160 | tf_op jit(solution)/shard_map/reduce_scatter | solution.py:340
  1021.2 36.7 %reduce-scatter.20.cloned.1.call-done = f32[128,768]{1,0:T(8,128)} async-done(((f32[128,3072]{1,0:T(8,128)}), f32[128,768]{1,0:T(8,128)}) %reduce-scatter.20.cloned.1.call-update) | async-done | bytes 393232 | tf_op jit(solution)/shard_map/reduce_scatter | solution.py:337
  1057.9 62.1 %reduce-scatter.16.cloned.1.call-done = f32[128,1536]{1,0:T(8,128)} async-done(((f32[128,6144]{1,0:T(8,128)}), f32[128,1536]{1,0:T(8,128)}) %reduce-scatter.16.cloned.1.call-update) | async-done | bytes 786448 | tf_op jit(solution)/shard_map/reduce_scatter | solution.py:336
  (367 shorter events, 406.4 us)
Async XLA Ops:
  7.2 42.2 %all-gather.16.cloned.1.call-start = ((), (), s32[]{:S(2)}) async-start(), calls=%async_computation.11 | async-start | bytes 1966080 | tf_op jit(solution)/shard_map/all_gather | solution.py:87
  8.0 114.5 %all-gather.18.cloned.1.call-start = ((), (), s32[]{:S(2)}) async-start(), calls=%async_computation.12 | async-start | bytes 14155776 | tf_op jit(solution)/shard_map/all_gather | solution.py:94
  49.5 120.4 %all-gather.20.cloned.1.call-start = ((), (), s32[]{:S(2)}) async-start(), calls=%async_computation.13 | async-start | bytes 7077888 | tf_op jit(solution)/shard_map/all_gather | solution.py:95
  68.1 199.5 %all-gather.24.cloned.1.call-start = ((), (), s32[]{:S(2)}) async-start(), calls=%async_computation.15 | async-start | bytes 4718592 | tf_op jit(solution)/shard_map/all_gather | solution.py:133
  179.7 100.7 %all-gather.22.cloned.1.call-start = ((), (), s32[]{:S(2)}) async-start(), calls=%async_computation.14 | async-start | bytes 4718592 | tf_op jit(solution)/shard_map/all_gather | solution.py:134
  181.9 161.9 %all-gather.26.cloned.1.call-start = ((), (), s32[]{:S(2)}) async-start(), calls=%async_computation.16 | async-start | bytes 2359296 | tf_op jit(solution)/shard_map/all_gather | solution.py:96
  196.6 155.7 %all-gather.30.cloned.1.call-start = ((), (), s32[]{:S(2)}) async-start(), calls=%async_computation.18 | async-start | bytes 4718592 | tf_op jit(solution)/shard_map/all_gather | solution.py:98
  213.0 150.3 %all-gather.28.cloned.1.call-start = ((), (), s32[]{:S(2)}) async-start(), calls=%async_computation.17 | async-start | bytes 4718592 | tf_op jit(solution)/shard_map/all_gather | solution.py:97
  229.9 245.4 %all-gather.32.cloned.1.call-start = ((), (), s32[]{:S(2)}) async-start(), calls=%async_computation.19 | async-start | bytes 4718592 | tf_op jit(solution)/shard_map/all_gather | solution.py:295
  256.3 225.5 %all-gather.34.cloned.1.call-start = ((), (), s32[]{:S(2)}) async-start(), calls=%async_computation.20 | async-start | bytes 4718592 | tf_op jit(solution)/shard_map/all_gather | solution.py:296
  382.5 249.4 %reduce-scatter.22.cloned.1.call-start = ((), (), s32[]{:S(2)}) async-start(), calls=%async_computation.26 | async-start | bytes 4718592 | tf_op jit(solution)/shard_map/reduce_scatter | solution.py:325
  385.3 247.2 %reduce-scatter.26.cloned.1.call-start = ((), (), s32[]{:S(2)}) async-start(), calls=%async_computation.28 | async-start | bytes 9437184 | tf_op jit(solution)/shard_map/reduce_scatter | solution.py:326
  391.1 255.2 %reduce-scatter.30.cloned.1.call-start = ((), (), s32[]{:S(2)}) async-start(), calls=%async_computation.30 | async-start | bytes 9437184 | tf_op jit(solution)/shard_map/reduce_scatter | solution.py:327
  401.3 341.2 %reduce-scatter.18.cloned.1.call-start = ((), (), s32[]{:S(2)}) async-start(), calls=%async_computation.24 | async-start | bytes 14155776 | tf_op jit(solution)/shard_map/reduce_scatter | solution.py:324
  592.1 311.2 %reduce-scatter.14.cloned.1.call-start = ((), (), s32[]{:S(2)}) async-start(), calls=%async_computation.22 | async-start | bytes 28311552 | tf_op jit(solution)/shard_map/reduce_scatter | solution.py:323
  618.1 321.8 %reduce-scatter.12.cloned.1.call-start = ((), (), s32[]{:S(2)}) async-start(), calls=%async_computation.21 | async-start | bytes 147456 | tf_op jit(solution)/shard_map/reduce_scatter | solution.py:333
  631.9 332.5 %reduce-scatter.24.cloned.1.call-start = ((), (), s32[]{:S(2)}) async-start(), calls=%async_computation.27 | async-start | bytes 655360 | tf_op jit(solution)/shard_map/reduce_scatter | solution.py:338
  632.5 359.9 %reduce-scatter.28.cloned.1.call-start = ((), (), s32[]{:S(2)}) async-start(), calls=%async_computation.29 | async-start | bytes 1310720 | tf_op jit(solution)/shard_map/reduce_scatter | solution.py:339
  632.6 487.5 %copy-start.1 = (f32[32,1024]{1,0:T(8,128)S(1)}, f32[32,1024]{1,0:T(8,128)}, u32[]{:S(2)}) copy-start(f32[32,1024]{1,0:T(8,128)} %param.27) | copy-start | bytes 393220
  632.6 274.4 %copy-start.38 = (f32[1024]{0:T(1024)S(1)}, f32[1024]{0:T(1024)}, u32[]{:S(2)}) copy-start(f32[1024]{0:T(1024)} %get-tuple-element.458) | copy-start | bytes 12292
  632.6 274.4 %copy-start.39 = (f32[1024]{0:T(1024)S(1)}, f32[1024]{0:T(1024)}, u32[]{:S(2)}) copy-start(f32[1024]{0:T(1024)} %get-tuple-element.462) | copy-start | bytes 12292
  633.1 388.1 %reduce-scatter.32.cloned.1.call-start = ((), (), s32[]{:S(2)}) async-start(), calls=%async_computation.31 | async-start | bytes 1310720 | tf_op jit(solution)/shard_map/reduce_scatter | solution.py:340
  646.3 411.6 %reduce-scatter.20.cloned.1.call-start = ((), (), s32[]{:S(2)}) async-start(), calls=%async_computation.25 | async-start | bytes 1966080 | tf_op jit(solution)/shard_map/reduce_scatter | solution.py:337
  742.5 377.5 %reduce-scatter.16.cloned.1.call-start = ((), (), s32[]{:S(2)}) async-start(), calls=%async_computation.23 | async-start | bytes 3932160 | tf_op jit(solution)/shard_map/reduce_scatter | solution.py:336
  (62 other events, 1832.2 us)
Sparse Core Ops, SparseCore 0:
  9.6 39.7 all-gather.15
  51.4 71.0 all-gather.17
  124.3 45.5 all-gather.19
  179.8 37.4 all-gather.23
  219.6 36.7 all-gather.21
  258.1 27.8 all-gather.25
  287.9 36.7 all-gather.29
  326.6 36.7 all-gather.27
  365.2 37.4 all-gather.31
  404.4 36.7 all-gather.33
  444.5 51.8 reduce-scatter.21
  500.1 71.2 reduce-scatter.25
  574.9 71.3 reduce-scatter.29
  650.1 92.3 reduce-scatter.17
  746.4 156.8 reduce-scatter.13
  906.4 33.3 reduce-scatter.11
  942.5 21.7 reduce-scatter.23
  967.1 25.2 reduce-scatter.27
  995.4 25.7 reduce-scatter.31
  1023.9 33.9 reduce-scatter.19
  1060.8 59.2 reduce-scatter.15
where the time goes:
time: 1140 us; the launch traced here: 1130 us
  waiting for transfers between devices  557 us (49%)
  matrix products  262 us (23%)
  blocking collectives  163 us (14%)
  local copies, waits for them, and re-layouts  83.3 us (7%)
  other arithmetic  30.5 us (3%)
  between operations  18 us (2%)
  starting transfers between devices  12.5 us (1%)
    reduce_scatter x1, waiting for transfers between devices, local(): lax.psum_scatter(g_ada, 'shard', scatter_dimension=0, tiled=True)  161 us
    reduce_scatter x1, waiting for transfers between devices, local(): lax.psum_scatter(g_qkv, 'shard', scatter_dimension=0, tiled=True)  96.1 us
    reduce_scatter x1, waiting for transfers between devices, local(): lax.psum_scatter(group_sums[0], 'grp', scatter_dimension=1, tiled=True)  62.1 us
    all_gather x1, waiting for transfers between devices, local(): lax.all_gather(w_ada, 'grp', axis=1, tiled=True)  41.5 us
    dot_general x8, matrix products, tile_step(): jnp.einsum('rhd,khd->hrk', query_heads, head_view(key_tile), preferred_el...  39.9 us
    reduce_scatter x1, waiting for transfers between devices, local(): lax.psum_scatter(group_sums[1], 'grp', scatter_dimension=1, tiled=True)  36.7 us
    all_gather x1, waiting for transfers between devices, local(): lax.all_gather(columns[1], 'shard', axis=0, tiled=True)  35.5 us
    all_gather x1, waiting for transfers between devices, local(): lax.all_gather(columns[0], 'shard', axis=0, tiled=True)  32.9 us
  transfers between devices with their start and end apart: 21, of which 13 were waited for; matrix products, arithmetic and copies ran while one was open for 31% of the time, Pallas kernels for 0%

commit v1 on v0

--- a/solution.py
+++ b/solution.py
@@ -3,6 +3,8 @@
 import jax
 import jax.numpy as jnp
 from jax import lax
+from jax.experimental import pallas as pl
+from jax.experimental.pallas import tpu as pltpu
 from jax.sharding import PartitionSpec as P
 
 D = 1024
@@ -54,7 +56,7 @@
     return tensor.reshape(tensor.shape[0], H, HD)
 
 
-def local(
+def local_any(
     frames,
     cotangent,
     seg_start,
@@ -361,6 +363,515 @@
     )
 
 
+LANES = 128
+SEPARATE = -(2.0**100)
+GELU_C = 0.7978845608028654
+GELU_A = 0.044715
+NT = (((1,), (1,)), ((), ()))
+TN = (((0,), (0,)), ((), ()))
+f32 = jnp.float32
+bf16 = jnp.bfloat16
+
+
+def dot(left, right, dims=(((1,), (0,)), ((), ()))):
+    return lax.dot_general(left, right, dims, preferred_element_type=f32)
+
+
+def params(limit_mib, steps=1):
+    return pltpu.CompilerParams(
+        dimension_semantics=("arbitrary",) * steps, vmem_limit_bytes=limit_mib * 2**20
+    )
+
+
+def moments(value):
+    centred = value - jnp.mean(value, axis=1, keepdims=True)
+    inv = lax.rsqrt(jnp.mean(centred * centred, axis=1, keepdims=True) + eps_norm)
+    return centred * inv, inv
+
+
+def norm_back(weighted, normal, inv):
+    return (
+        weighted
+        - jnp.mean(weighted, axis=1, keepdims=True)
+        - normal * jnp.mean(weighted * normal, axis=1, keepdims=True)
+    ) * inv
+
+
+def swap_halves(value):
+    lane = lax.broadcasted_iota(jnp.int32, value.shape, 1)
+    return jnp.where(lane % HD < HD // 2, pltpu.roll(value, 96, 1), pltpu.roll(value, 32, 1))
+
+
+def members(seg_ref, block, rows):
+    place = block * rows + lax.broadcasted_iota(jnp.int32, (rows, 1), 0)
+    out = []
+    for slot in range(3):
+        begin = seg_ref[block, slot]
+        inside = (place >= begin) & (place < begin + seg_ref[block, 3 + slot])
+        out.append(inside.astype(f32))
+    return out
+
+
+def mod_rows(table_ref, seg_ref, block, member, part):
+    total = None
+    for slot in range(3):
+        row = table_ref[pl.ds(seg_ref[block, 6 + slot], 1), pl.ds(part * D, D)]
+        term = member[slot] * row
+        total = term if total is None else total + term
+    return total
+
+
+def slot_sums(member, value):
+    return [jnp.sum(column * value, axis=0, keepdims=True) for column in member]
+
+
+def qkv_kernel(seg_ref, x_ref, table_ref, w_ref, b_ref, cos_ref, sin_ref, q_ref, k_ref, v_ref, h_ref):
+    block = pl.program_id(0)
+    last = pl.num_programs(0) - 1
+    rows = x_ref.shape[0]
+    member = members(seg_ref, block, rows)
+    normal, _ = moments(x_ref[...].astype(f32))
+    shift = mod_rows(table_ref, seg_ref, block, member, 0)
+    scale = mod_rows(table_ref, seg_ref, block, member, 1)
+    hidden = (normal * (1.0 + scale) + shift).astype(bf16)
+    h_ref[...] = hidden
+    projected = dot(hidden, w_ref[...]) + b_ref[...]
+    cosine, sine = cos_ref[...], sin_ref[...]
+    turned = []
+    for part in range(2):
+        piece = projected[:, part * LANES : (part + 1) * LANES]
+        turned.append(piece * cosine + swap_halves(piece) * sine)
+    queries = turned[0].astype(bf16).astype(f32) * 0.125
+    keys = turned[1]
+    values = projected[:, 2 * LANES :]
+    lane = lax.broadcasted_iota(jnp.int32, (rows, LANES), 1)
+    place = block * rows + lax.broadcasted_iota(jnp.int32, (rows, 1), 0)
+    query_extra = jnp.zeros((rows, LANES), f32)
+    key_extra = jnp.zeros((rows, LANES), f32)
+    for index in range(6):
+        where, slot = (0, index) if index < 3 else (last, index - 3)
+        begin = seg_ref[where, slot]
+        inside = (place >= begin) & (place < begin + seg_ref[where, 3 + slot])
+        here = lane == HD + index
+        query_extra = jnp.where(here, jnp.where(inside, 0.0, SEPARATE), query_extra)
+        key_extra = jnp.where(here, jnp.where(inside, 1.0, 0.0), key_extra)
+    value_extra = jnp.where((lane >= HD) & (lane < HD + 3), 1.0, 0.0)
+    low = lane < HD
+    for head in range(2):
+        for ref, value, extra in (
+            (q_ref, queries, query_extra),
+            (k_ref, keys, key_extra),
+            (v_ref, values, value_extra),
+        ):
+            own = value if head == 0 else pltpu.roll(value, HD, 1)
+            ref[head] = jnp.where(low, own, extra).astype(bf16)
+
+
+def attend_kernel(q_ref, k_ref, v_ref, o_ref, mixed_ref, l_ref):
+    keys_in_all = k_ref.shape[1]
+    tile = 512
+    ratios, sums = [], []
+    for head in range(2):
+        query = q_ref[head]
+        total = None
+        for at in range(0, keys_in_all, tile):
+            expo = jnp.exp(dot(query, k_ref[head, at : at + tile], NT))
+            term = dot(expo.astype(bf16), v_ref[head, at : at + tile])
+            total = term if total is None else total + term
+        norm = total[:, HD : HD + 1]
+        ratios.append(total / norm)
+        sums.append(norm)
+    lane = lax.broadcasted_iota(jnp.int32, ratios[0].shape, 1)
+    mixed = jnp.where(lane < HD, ratios[0], pltpu.roll(ratios[1], HD, 1))
+    mixed_ref[...] = mixed
+    o_ref[...] = mixed.astype(bf16)
+    l_ref[...] = jnp.where(lane < HD, sums[0], sums[1])
+
+
+def block_kernel(
+    base_ref, seg_ref, x_ref, cot_ref, o_ref, table_ref, w_ref, b_out_ref, b_up_ref, b_down_ref,
+    out_ref, dx1_ref, do_ref, h2_ref, du_ref, act_ref, dff_ref, da_ref, slots_ref, gb_out_ref, gb_up_ref, gb_down_ref,
+):
+    rows = x_ref.shape[0]
+    shards, groups = w_ref.shape[:2]
+    block = base_ref[0]
+    member = members(seg_ref, block, rows)
+    modulation = partial(mod_rows, table_ref, seg_ref, block, member)
+    wide = D // groups
+
+    def weight(group, start):
+        return w_ref[:, group, start : start + LANES, :].reshape(D, wide)
+
+    def weight_down(group):
+        return w_ref[:, group, 0 : 2 * LANES, :].reshape(2 * D, wide)
+
+    mixed = jnp.concatenate([o_ref[shard] for shard in range(shards)], axis=1)
+    attn = jnp.concatenate([dot(mixed, weight(group, 256)) for group in range(groups)], axis=1)
+    attn = attn + b_out_ref[...]
+    gate1 = modulation(2)
+    after = x_ref[...].astype(f32) + gate1 * attn
+    normal, inv = moments(after)
+    scale2 = 1.0 + modulation(4)
+    hidden = (normal * scale2 + modulation(3)).astype(bf16)
+    h2_ref[...] = hidden
+    up = [dot(hidden, weight(group, start)) for group in range(groups) for start in (384, 512)]
+    up = jnp.concatenate(up, axis=1) + b_up_ref[...]
+    inner = jnp.tanh(GELU_C * (up + GELU_A * (up * up * up)))
+    act = (0.5 * up * (1.0 + inner)).astype(bf16)
+    act_ref[...] = act
+    slope = 0.5 * (1.0 + inner) + (0.5 * GELU_C) * up * (1.0 - inner * inner) * (
+        1.0 + (3.0 * GELU_A) * up * up
+    )
+    branch = jnp.concatenate([dot(act, weight_down(group)) for group in range(groups)], axis=1)
+    branch = branch + b_down_ref[...]
+    gate2 = modulation(5)
+    out_ref[...] = (after + gate2 * branch).astype(bf16)
+
+    cot = cot_ref[...].astype(f32)
+    dff = (gate2 * cot).astype(bf16)
+    dff_ref[...] = dff
+    gb_down_ref[...] = jnp.sum(dff.astype(f32), axis=0, keepdims=True)
+    d_gate2 = slot_sums(member, cot * branch)
+    d_act = sum(dot(dff[:, g * wide : (g + 1) * wide], weight_down(g), NT) for g in range(groups))
+    du = (d_act * slope).astype(bf16)
+    du_ref[...] = du
+    gb_up_ref[...] = jnp.sum(du.astype(f32), axis=0, keepdims=True)
+    d_hidden = None
+    for index in range(2 * groups):
+        piece = du[:, index * wide : (index + 1) * wide]
+        term = dot(piece, weight(index // 2, 384 + 128 * (index % 2)), NT)
+        d_hidden = term if d_hidden is None else d_hidden + term
+    d_shift2 = slot_sums(member, d_hidden)
+    d_scale2 = slot_sums(member, d_hidden * normal)
+    d_after = cot + norm_back(d_hidden * scale2, normal, inv)
+    dx1_ref[...] = d_after
+    d_gate1 = slot_sums(member, d_after * attn)
+    da = (gate1 * d_after).astype(bf16)
+    da_ref[...] = da
+    gb_out_ref[...] = jnp.sum(da.astype(f32), axis=0, keepdims=True)
+    d_mixed = sum(dot(da[:, g * wide : (g + 1) * wide], weight(g, 256), NT) for g in range(groups))
+    d_mixed = d_mixed.astype(bf16)
+    for shard in range(shards):
+        do_ref[shard] = d_mixed[:, shard * LANES : (shard + 1) * LANES]
+    slots_ref[...] = jnp.concatenate(d_gate1 + d_shift2 + d_scale2 + d_gate2, axis=0)
+
+
+def weight_grad_kernel(o_ref, da_ref, h2_ref, du_ref, act_ref, dff_ref, g_ref):
+    shards = o_ref.shape[0]
+    wide = g_ref.shape[3]
+    g_ref[:, 0, 0:256, :] = dot(act_ref[...], dff_ref[...], TN).astype(bf16).reshape(shards, 256, wide)
+    mixed = jnp.concatenate([o_ref[shard] for shard in range(shards)], axis=1)
+    g_ref[:, 0, 256:384, :] = dot(mixed, da_ref[...], TN).astype(bf16).reshape(shards, LANES, wide)
+    for half in range(2):
+        piece = dot(h2_ref[...], du_ref[:, half * wide : (half + 1) * wide], TN).astype(bf16)
+        start = 384 + 128 * half
+        g_ref[:, 0, start : start + 128, :] = piece.reshape(shards, LANES, wide)
+
+
+def attend_back_kernel(
+    q_ref, k_ref, v_ref, do_ref, mixed_ref, l_ref, cos_ref, sin_ref, dq_ref, dk_ref, dv_ref, gb_ref, dn, dq_t
+):
+    step = pl.program_id(0)
+    rows = k_ref.shape[1]
+    frames = q_ref.shape[1]
+    tile = 512
+    lane = lax.broadcasted_iota(jnp.int32, (rows, LANES), 1)
+    low = lane < HD
+
+    @pl.when(step == 0)
+    def _():
+        gb_ref[...] = jnp.zeros_like(gb_ref)
+        dq_t[...] = jnp.zeros_like(dq_t)
+        for at in range(0, frames, rows):
+            here = slice(at, at + rows)
+            d_out = do_ref[here].astype(f32)
+            norm = l_ref[here]
+            d_num = (d_out / norm).astype(bf16).astype(f32)
+            both = d_out * mixed_ref[here]
+            for head in range(2):
+                mine = low if head == 0 else ~low
+                total = jnp.sum(jnp.where(mine, both, 0.0), axis=1, keepdims=True)
+                delta = -total / norm[:, head * HD : head * HD + 1]
+                first = delta.astype(bf16).astype(f32)
+                second = (delta - first).astype(bf16).astype(f32)
+                third = delta - first - second
+                extra = jnp.where(lane == HD, first, jnp.where(lane == HD + 1, second, third))
+                extra = jnp.where(lane < HD + 3, extra, 0.0)
+                own = d_num if head == 0 else pltpu.roll(d_num, HD, 1)
+                dn[head, here] = jnp.where(low, own, extra).astype(bf16)
+
+    d_keys, d_values = [], []
+    for head in range(2):
+        key, value = k_ref[head], v_ref[head]
+        key_t = key.T
+        dk_total, dv_total = None, None
+        for at in range(0, frames, tile):
+            here = slice(at, at + tile)
+            query, d_num = q_ref[head, here], dn[head, here]
+            expo = jnp.exp(dot(key, query, NT))
+            d_score = (expo * dot(value, d_num, NT)).astype(bf16)
+            dk_term = dot(d_score, query)
+            dv_term = dot(expo.astype(bf16), d_num)
+            dk_total = dk_term if dk_total is None else dk_total + dk_term
+            dv_total = dv_term if dv_total is None else dv_total + dv_term
+            dq_t[head, :, here] += dot(key_t, d_score)
+        d_keys.append(dk_total)
+        d_values.append(dv_total)
+
+    def both_heads(pair):
+        return jnp.where(low, pair[0], pltpu.roll(pair[1], HD, 1))
+
+    def turn_back(value, here):
+        return (value * cos_ref[here] - swap_halves(value) * sin_ref[here]).astype(bf16)
+
+    here = pl.ds(pl.multiple_of(step * rows, rows), rows)
+    d_key = turn_back(both_heads(d_keys), here)
+    d_value = both_heads(d_values).astype(bf16)
+    dk_ref[...] = d_key
+    dv_ref[...] = d_value
+    gb_ref[1:2] += jnp.sum(d_key.astype(f32), axis=0, keepdims=True)
+    gb_ref[2:3] += jnp.sum(d_value.astype(f32), axis=0, keepdims=True)
+
+    @pl.when(step == pl.num_programs(0) - 1)
+    def _():
+        for at in range(0, frames, rows):
+            part = slice(at, at + rows)
+            d_query = both_heads([0.125 * dq_t[head, :, part].T for head in range(2)])
+            d_query = turn_back(d_query, part)
+            dq_ref[part] = d_query
+            gb_ref[0:1] += jnp.sum(d_query.astype(f32), axis=0, keepdims=True)
+
+
+def input_grad_kernel(base_ref, seg_ref, d_ref, w_ref, x_ref, dx1_ref, table_ref, grad_ref, slots_ref):
+    block = base_ref[0]
+    rows = x_ref.shape[0]
+    member = members(seg_ref, block, rows)
+    scale = 1.0 + mod_rows(table_ref, seg_ref, block, member, 1)
+    d_hidden = sum(dot(d_ref[shard], w_ref[shard], NT) for shard in range(d_ref.shape[0]))
+    normal, inv = moments(x_ref[...].astype(f32))
+    grad_ref[...] = dx1_ref[...] + norm_back(d_hidden * scale, normal, inv)
+    sums = slot_sums(member, d_hidden) + slot_sums(member, d_hidden * normal)
+    slots_ref[...] = jnp.concatenate(sums + [jnp.zeros((2, D), f32)], axis=0)
+
+
+def exchange(pieces, axis, size):
+    own = lax.axis_index(axis)
+    out = [lax.dynamic_index_in_dim(pieces, own, 0, keepdims=False)]
+    for step in range(1, size):
+        block = lax.dynamic_index_in_dim(pieces, (own - step) % size, 0, keepdims=False)
+        out.append(lax.ppermute(block, axis, [(i, (i - step) % size) for i in range(size)]))
+    return out
+
+
+def shape(*dims, kind=bf16):
+    return jax.ShapeDtypeStruct(dims, kind)
+
+
+def whole(*dims):
+    return pl.BlockSpec(dims, lambda *_: (0,) * len(dims))
+
+
+smem = pl.BlockSpec(memory_space=pltpu.SMEM)
+
+
+def local_heads(
+    groups, shards, frames, cotangent, seg_start, seg_length, seg_step, time_table,
+    w_ada, b_ada, w_qkv, b_qkv, w_out, b_out, w_up, b_up, w_down, b_down,
+):
+    rows = frames.shape[0]
+    packed = rows * shards
+    steps = time_table.shape[0]
+    shard = lax.axis_index("shard")
+    depth = D // shards
+    wide = D // groups
+
+    frames_all = lax.all_gather(frames, "shard", axis=0, tiled=True)
+    w_cols = lax.all_gather(w_qkv, "grp", axis=1, tiled=True)
+    w_cols = w_cols.reshape(depth, 3, shards, LANES).transpose(2, 0, 1, 3).reshape(shards, depth, 3 * LANES)
+    w_heads = lax.all_to_all(w_cols, "shard", split_axis=0, concat_axis=0, tiled=True).reshape(D, 3 * LANES)
+
+    activated = jax.nn.silu(time_table).astype(bf16)
+    act_own = lax.dynamic_slice_in_dim(activated, shard * depth, depth, 1)
+    partial_mod = dot(act_own, w_ada)
+    mod_wide = partial_mod.shape[1]
+    segs = jnp.concatenate((seg_start, seg_length, seg_step), axis=1).astype(f32)
+    biases = [b.astype(f32) for b in (b_ada, b_qkv, b_out, b_up, b_down)]
+    sizes = [b.shape[0] for b in biases]
+    extra = jnp.concatenate(biases + [segs[0]])
+    extra_rows = -(-extra.shape[0] // mod_wide)
+    extra = jnp.pad(extra, (0, extra_rows * mod_wide - extra.shape[0])).reshape(extra_rows, mod_wide)
+    small = lax.all_gather(jnp.concatenate((partial_mod, extra), axis=0), "shard", axis=0)
+    mod_own = jnp.sum(small[:, :steps], axis=0)
+    extra = small[:, steps:].reshape(shards, extra_rows * mod_wide)
+    full, at = [], 0
+    for size in sizes:
+        full.append(extra[:, at : at + size].reshape(1, shards * size))
+        at += size
+    ada_bias, qkv_bias, out_bias, up_bias, down_bias = full
+    seg_all = extra[:, at : at + 9].astype(jnp.int32)
+    table = lax.all_gather(mod_own, "grp", axis=1, tiled=True) + ada_bias
+    qkv_bias = lax.dynamic_index_in_dim(qkv_bias.reshape(3, shards, LANES), shard, 1, keepdims=False)
+    qkv_bias = qkv_bias.reshape(1, 3 * LANES)
+
+    place = jnp.arange(packed, dtype=jnp.int32).reshape(shards, rows)
+    begin = seg_all[:, None, 0:3]
+    inside = (place[:, :, None] >= begin) & (place[:, :, None] < begin + seg_all[:, None, 3:6])
+    seg_low = jnp.sum(jnp.where(inside, begin, 0), axis=2)
+    cosine, sine = angles((place - seg_low).astype(f32).reshape(packed))
+    cosine = jnp.tile(cosine, (1, 4))
+    sine = jnp.concatenate((-sine, sine, -sine, sine), axis=1)
+
+    by_block = lambda width: pl.BlockSpec((rows, width), lambda i: (i, 0))
+    two_heads = pl.BlockSpec((2, rows, LANES), lambda i: (0, i, 0))
+    q, k, v, h1_all = pl.pallas_call(
+        qkv_kernel,
+        grid=(shards,),
+        in_specs=[
+            smem, by_block(D), whole(steps, 2 * D), whole(D, 3 * LANES), whole(1, 3 * LANES),
+            by_block(LANES), by_block(LANES),
+        ],
+        out_specs=[two_heads, two_heads, two_heads, by_block(D)],
+        out_shape=[shape(2, packed, LANES)] * 3 + [shape(packed, D)],
+        compiler_params=params(40),
+        cost_estimate=pl.CostEstimate(flops=2 * packed * D * 384, bytes_accessed=2 * packed * D * 4, transcendentals=0),
+        name="qkv",
+    )(seg_all, frames_all, table[:, : 2 * D], w_heads, qkv_bias, cosine, sine)
+
+    attn_flops = 2 * 2 * packed * packed * 256
+    o_heads, mixed, norm = pl.pallas_call(
+        attend_kernel,
+        grid=(shards,),
+        in_specs=[two_heads, whole(2, packed, LANES), whole(2, packed, LANES)],
+        out_specs=[by_block(LANES)] * 3,
+        out_shape=[shape(packed, LANES), shape(packed, LANES, kind=f32), shape(packed, LANES, kind=f32)],
+        compiler_params=params(40),
+        cost_estimate=pl.CostEstimate(flops=2 * attn_flops, bytes_accessed=2**22, transcendentals=2 * packed * packed),
+        name="attend",
+    )(q, k, v)
+
+    pack = jnp.concatenate((w_down, w_out, w_up[:, :wide], w_up[:, wide:]), axis=0)
+    pack_rows = pack.shape[0]
+    weights = lax.all_gather(lax.all_gather(pack, "grp", axis=0), "shard", axis=0)
+
+    o = lax.all_to_all(o_heads.reshape(shards, rows, LANES), "shard", split_axis=0, concat_axis=0, tiled=True)
+    base = shard.astype(jnp.int32).reshape(1)
+    block_flops = 2 * rows * D * D * 10
+    out, dx1, d_mixed, h2, du, act, dff, da, slots_ff, gb_out, gb_up, gb_down = pl.pallas_call(
+        block_kernel,
+        in_specs=[smem, smem] + [pl.BlockSpec(memory_space=pltpu.VMEM)] * 8,
+        out_specs=[pl.BlockSpec(memory_space=pltpu.VMEM)] * 12,
+        out_shape=[
+            shape(rows, D), shape(rows, D, kind=f32), shape(shards, rows, LANES), shape(rows, D), shape(rows, 2 * D),
+            shape(rows, 2 * D), shape(rows, D), shape(rows, D), shape(12, D, kind=f32),
+            shape(1, D, kind=f32), shape(1, 2 * D, kind=f32), shape(1, D, kind=f32),
+        ],
+        compiler_params=pltpu.CompilerParams(vmem_limit_bytes=56 * 2**20),
+        cost_estimate=pl.CostEstimate(flops=block_flops, bytes_accessed=2**24, transcendentals=rows * 2 * D),
+        name="block",
+    )(base, seg_all, frames, cotangent, o, table, weights, out_bias, up_bias, down_bias)
+
+    d_heads = lax.all_to_all(d_mixed, "shard", split_axis=0, concat_axis=0, tiled=True).reshape(packed, LANES)
+
+    by_group = lambda width: pl.BlockSpec((rows, width), lambda i: (0, i))
+    grad_pack = pl.pallas_call(
+        weight_grad_kernel,
+        grid=(groups,),
+        in_specs=[
+            whole(shards, rows, LANES), by_group(wide), whole(rows, D), by_group(2 * wide), whole(rows, 2 * D), by_group(wide),
+        ],
+        out_specs=pl.BlockSpec((shards, 1, pack_rows, wide), lambda i: (0, i, 0, 0)),
+        out_shape=shape(shards, groups, pack_rows, wide),
+        compiler_params=params(40),
+        cost_estimate=pl.CostEstimate(flops=block_flops // 2, bytes_accessed=2**24, transcendentals=0),
+        name="weight_grads",
+    )(o, da, h2, du, act, dff)
+    grad_pack = lax.psum_scatter(grad_pack, "shard", scatter_dimension=0, tiled=False)
+    grad_pack = lax.psum_scatter(grad_pack, "grp", scatter_dimension=0, tiled=False).astype(f32)
+    g_down = grad_pack[: 2 * LANES]
+    g_out = grad_pack[2 * LANES : 3 * LANES]
+    g_up = jnp.concatenate((grad_pack[3 * LANES : 4 * LANES], grad_pack[4 * LANES :]), axis=1)
+
+    dq, dk, dv, gb_qkv = pl.pallas_call(
+        attend_back_kernel,
+        grid=(shards,),
+        in_specs=[
+            whole(2, packed, LANES), two_heads, two_heads, whole(packed, LANES), whole(packed, LANES),
+            whole(packed, LANES), whole(packed, LANES), whole(packed, LANES),
+        ],
+        out_specs=[whole(packed, LANES), by_block(LANES), by_block(LANES), whole(3, LANES)],
+        out_shape=[shape(packed, LANES)] * 3 + [shape(3, LANES, kind=f32)],
+        scratch_shapes=[pltpu.VMEM((2, packed, LANES), bf16), pltpu.VMEM((2, LANES, packed), f32)],
+        compiler_params=params(48),
+        cost_estimate=pl.CostEstimate(flops=5 * attn_flops, bytes_accessed=2**23, transcendentals=2 * packed * packed),
+        name="attend_back",
+    )(q, k, v, d_heads, mixed, norm, cosine, sine)
+
+    d_own = jnp.concatenate((dq, dk, dv), axis=1)
+    d_rows = lax.all_to_all(d_own.reshape(shards, rows, 3 * LANES), "shard", split_axis=0, concat_axis=0, tiled=True)
+    w_all = lax.all_gather(w_heads, "shard", axis=0)
+    grad_frames, slots_qkv = pl.pallas_call(
+        input_grad_kernel,
+        in_specs=[smem, smem] + [pl.BlockSpec(memory_space=pltpu.VMEM)] * 5,
+        out_specs=[pl.BlockSpec(memory_space=pltpu.VMEM)] * 2,
+        out_shape=[shape(rows, D, kind=f32), shape(8, D, kind=f32)],
+        compiler_params=pltpu.CompilerParams(vmem_limit_bytes=40 * 2**20),
+        cost_estimate=pl.CostEstimate(flops=2 * rows * D * 3 * D, bytes_accessed=2**23, transcendentals=0),
+        name="input_grad",
+    )(base, seg_all, d_rows, w_all, frames, dx1, table[:, : 2 * D])
+
+    g_heads = dot(h1_all, d_own, TN).astype(bf16).reshape(shards, depth, 3 * LANES)
+    g_rows = lax.all_to_all(g_heads, "shard", split_axis=0, concat_axis=0, tiled=True)
+    g_rows = g_rows.reshape(shards, depth, 3, LANES).transpose(1, 2, 0, 3).reshape(depth, groups, 3 * D // groups)
+    g_qkv = sum(piece.astype(f32) for piece in exchange(g_rows.transpose(1, 0, 2), "grp", groups))
+
+    d_slot = jnp.concatenate((slots_qkv[:6], slots_ff), axis=0).reshape(6, 3, D).transpose(1, 0, 2).reshape(3, 6 * D)
+    row_sums = jnp.concatenate((gb_qkv.reshape(-1), gb_out[0], gb_up[0], gb_down[0]))
+    sum_rows = -(-row_sums.shape[0] // (6 * D))
+    row_sums = jnp.pad(row_sums, (0, sum_rows * 6 * D - row_sums.shape[0])).reshape(sum_rows, 6 * D)
+    tail = lax.all_gather(jnp.concatenate((d_slot, row_sums), axis=0), "shard", axis=0)
+    d_slots = tail[:, :3]
+    d_segs = jnp.concatenate(
+        (d_slots[0], d_slots[shards - 1], jnp.sum(d_slots[1 : shards - 1], axis=(0, 1))[None]), axis=0
+    )
+    step_ids = jnp.concatenate((seg_all[0, 6:], seg_all[shards - 1, 6:], jnp.sum(seg_all[1, 6:])[None])).astype(f32)
+    rest = tail[:, 3:].reshape(shards, sum_rows * 6 * D)
+    gb_heads = rest[:, : 3 * LANES].reshape(shards, 3, LANES).transpose(1, 0, 2).reshape(3 * D)
+    others = jnp.sum(rest[:, 3 * LANES : 3 * LANES + 4 * D], axis=0)
+    sums = (
+        jnp.sum(d_segs, axis=0), gb_heads, others[:D], others[D : 3 * D], others[3 * D : 4 * D],
+    )
+    own_sums = [lax.dynamic_slice_in_dim(total, shard * size, size) for total, size in zip(sums, sizes)]
+    send = jnp.concatenate(own_sums + [step_ids])
+    send_rows = -(-send.shape[0] // mod_wide)
+    send = jnp.pad(send, (0, send_rows * mod_wide - send.shape[0])).reshape(1, send_rows, mod_wide)
+    parts = jnp.concatenate(
+        (d_segs.reshape(7, groups, mod_wide).transpose(1, 0, 2), jnp.broadcast_to(send, (groups, send_rows, mod_wide))), axis=1
+    )
+    parts = exchange(parts, "grp", groups)
+    d_rows_all = jnp.concatenate([piece[:7] for piece in parts], axis=0)
+    rest = [piece[7:].reshape(-1) for piece in parts]
+    at = sum(sizes)
+    ids = jnp.concatenate([piece[at : at + 7] for piece in rest])
+    onehot = (ids[None, :] == jnp.arange(steps, dtype=f32)[:, None]).astype(f32)
+    d_table = jnp.dot(onehot, d_rows_all, precision=top_precision)
+    g_ada = jnp.dot(act_own.astype(f32).T, d_table, precision=top_precision)
+    bias_sums = sum(piece[:at] for piece in rest)
+    bias_grads, start = [], 0
+    for size in sizes:
+        bias_grads.append(bias_sums[start : start + size])
+        start += size
+    gb_ada, gb_qkv, gb_out, gb_up, gb_down = bias_grads
+
+    d_act = lax.dot_general(d_table, w_ada.astype(f32), NT, precision=top_precision, preferred_element_type=f32)
+    table_own = lax.dynamic_slice_in_dim(time_table, shard * depth, depth, 1)
+    g_table = jax.vjp(jax.nn.silu, table_own)[1](d_act)[0]
+    for_all = jnp.broadcast_to(g_table[None], (groups,) + g_table.shape)
+    g_table = sum(exchange(for_all, "grp", groups))
+    return (
+        out, grad_frames, g_table, g_ada, gb_ada, g_qkv, gb_qkv, g_out, gb_out, g_up, gb_up, g_down, gb_down,
+    )
+
+
 def solution(mesh):
     in_specs = (
         P(("grp", "shard"), None),
@@ -395,4 +906,6 @@
         P("shard", "grp"),
         P("shard"),
     )
+    by_heads = mesh.shape["shard"] * 2 * HD == D
+    local = partial(local_heads, mesh.shape["grp"], mesh.shape["shard"]) if by_heads else local_any
     return jax.shard_map(local, mesh=mesh, in_specs=in_specs, out_specs=out_specs, check_vma=False)

time: 1140 us -> 400 us (0.35); the launches traced: 1130 us -> 399 us
  waiting for transfers between devices: 557 us -> 97.8 us
  matrix products: 262 us -> 7.84 us
  Pallas kernels: 0 us -> 88.2 us
  blocking collectives: 163 us -> 108 us
  local copies, waits for them, and re-layouts: 83.3 us -> 32.9 us
  starting transfers between devices: 12.5 us -> 24 us
    reduce_scatter x11 -> x2, waiting for transfers between devices: 439 us -> 1.15 us  [the longest x1 1.15 us: local_heads(): lax.psum_scatter(grad_pack, 'grp', scatter_dimension=0, tiled=False)]
    dot_general x47 -> x5, matrix products: 262 us -> 7.84 us  [the longest x2 4.22 us: dot(): return lax.dot_general(left, right, dims, preferred_element_type=f32)]
    pallas_call x0 -> x6, Pallas kernels: none -> 88.2 us  [the longest x1 34.6 us: local_heads(): pl.pallas_call(attend_back_kernel, grid=(shards,), in_specs=[whole(2, pac...]
    all_gather x10 -> x3, blocking collectives: 120 us -> 47 us  [the longest x1 19.4 us: local_heads(): table = lax.all_gather(mod_own, 'grp', axis=1, tiled=True) + ada_bias]
    all_gather x10 -> x5, waiting for transfers between devices: 116 us -> 54.4 us  [the longest x1 29 us: local_heads(): lax.all_gather(pack, 'grp', axis=0)]
    all_to_all x0 -> x3, blocking collectives: none -> 60.9 us  [the longest x1 24.4 us: local_heads(): lax.all_to_all(g_heads, 'shard', split_axis=0, concat_axis=0, tiled=True)]
    dynamic_slice x40 -> x0, local copies, waits for them, and re-layouts: 32.9 us -> none  [the longest x32 32.8 us: local(): lax.scan(tile_step, (zero_heads, jnp.zeros((frame_rows, H), jnp.float32))...]
    all_to_all x0 -> x2, waiting for transfers between devices: none -> 28.8 us  [the longest x1 16 us: local_heads(): lax.all_to_all(d_own.reshape(shards, rows, 3 * LANES), 'shard', split_axi...]
  transfers between devices with their start and end apart: 21 -> 18, of which waited for: 13 -> 8; matrix products, arithmetic and copies ran while one was open for 31% -> 11% of each run, Pallas kernels for 0% -> 22%
where the time goes in v1:
time: 400 us; the launch traced here: 399 us
  blocking collectives  108 us (27%)
  waiting for transfers between devices  97.8 us (24%)
  Pallas kernels  88.2 us (22%)
  local copies, waits for them, and re-layouts  32.9 us (8%)
  other arithmetic  25.1 us (6%)
  starting transfers between devices  24 us (6%)
  between operations  14.9 us (4%)
  matrix products  7.84 us (2%)
    pallas_call x1, Pallas kernels, local_heads(): pl.pallas_call(attend_back_kernel, grid=(shards,), in_specs=[whole(2, pac...  34.6 us
    all_gather x1, waiting for transfers between devices, local_heads(): lax.all_gather(pack, 'grp', axis=0)  29 us
    all_to_all x1, blocking collectives, local_heads(): lax.all_to_all(g_heads, 'shard', split_axis=0, concat_axis=0, tiled=True)  24.4 us
    all_gather x1, waiting for transfers between devices, local_heads(): lax.all_gather(lax.all_gather(pack, 'grp', axis=0), 'shard', axis=0)  21.2 us
    unnamed x92, local copies, waits for them, and re-layouts  20.7 us
    all_gather x1, blocking collectives, local_heads(): table = lax.all_gather(mod_own, 'grp', axis=1, tiled=True) + ada_bias  19.4 us
    all_to_all x1, blocking collectives, local_heads(): lax.all_to_all(d_mixed, 'shard', split_axis=0, concat_axis=0, tiled=True)  18.3 us
    all_gather x1, blocking collectives, local_heads(): w_cols = lax.all_gather(w_qkv, 'grp', axis=1, tiled=True)  18.2 us
  transfers between devices with their start and end apart: 18, of which 8 were waited for; matrix products, arithmetic and copies ran while one was open for 11% of the time, Pallas kernels for 22%

profile of v1, /device:TPU:0, one launch (start us, length us, event | category | flops | bytes accessed | tf_op | source)
XLA Modules:
  0.0 398.6 jit_solution(6441101703627107381)
XLA Ops:
  16.6 29.0 %all-gather.16.cloned.1.call-done = bf16[2560,256]{1,0:T(8,128)(2,1)} async-done(((bf16[640,256]{1,0:T(8,128)(2,1)}), bf16[2560,256]{1,0:T(8,128)(2,1)}) %all-gather.16.cloned.1.call-update) | async-done | bytes 1310736 | tf_op jit(solution)/shard_map/all_gather | solution.py:754
  45.8 18.2 %all_gather.40 = bf16[128,3072]{0,1:T(8,128)(2,1)S(1)} all-gather(bf16[128,768]{0,1:T(8,128)(2,1)S(1)} %copy.79), channel_id=1, replica_groups=mesh['grp'=4,'shard'=8] {'grp'}, dimensions={1}, use_global_device_ids=true | all-gather | bytes 983040 | tf_op jit(solution)/shard_map/all_gather | solution.py:689
  64.1 18.1 %all_to_all.25 = bf16[8,128,384]{1,2,0:T(8,128)(2,1)S(1)} all-to-all(bf16[8,128,384]{1,2,0:T(8,128)(2,1)S(1)} %bitcast.110), channel_id=1, replica_groups=mesh['grp'=4,'shard'=8] {'shard'}, dimensions={0} | all-to-all | bytes 1572864 | tf_op jit(solution)/shard_map/all_to_all | solution.py:691
  85.5 5.5 %fusion.2 = (f32[2048,32]{1,0:T(8,128)}, f32[2048,32]{1,0:T(8,128)}, f32[2048,32]{1,0:T(8,128)S(1)}) fusion(f32[32]{0:T(128)S(1)} %multiply_power_fusion, f32[2048]{0:T(1024)S(1)} %bitcast.131), kind=kLoop, calls=%fused_computation.14 | loop fusion | flops 131072 | bytes 794752 | tf_op jit(solution)/shard_map/neg | solution.py:722
  93.7 19.4 %all_gather.39 = f32[32,6144]{1,0:T(8,128)S(1)} all-gather(f32[32,1536]{1,0:T(8,128)S(1)} %slice_reduce_fusion), channel_id=1, replica_groups=mesh['grp'=4,'shard'=8] {'grp'}, dimensions={1}, use_global_device_ids=true | all-gather | bytes 983040 | tf_op jit(solution)/shard_map/all_gather | solution.py:712
  117.3 4.2 %all-gather.12.cloned.1.call-done.x_ref = bf16[2048,1024]{1,0:T(8,128)(2,1)} async-done(((bf16[256,1024]{1,0:T(8,128)(2,1)}), bf16[2048,1024]{1,0:T(8,128)(2,1)}) %all-gather.12.cloned.1.call-update) | async-done | bytes 4194320 | tf_op jit(solution)/shard_map/all_gather | solution.py:688
  121.5 12.2 %qkv.1 = (bf16[2,2048,128]{2,1,0:T(8,128)(2,1)S(1)}, bf16[2,2048,128]{2,1,0:T(8,128)(2,1)S(1)}, bf16[2,2048,128]{2,1,0:T(8,128)(2,1)S(1)}, bf16[2048,1024]{1,0:T(8,128)(2,1)S(1)}) custom-call(s32[8,9]{1,0:T(8,128)S(1)} %slice_convert_fusion.seg_ref, bf16[2048,1024]{1,0:T(8,128)(2,1)} %all-gather.12.cloned.1.call-done.x_ref, ...), custom_call_target="tpu_custom_call" | custom-call | flops 1610612736 | bytes 16777216 | tf_op jit(solution)/shard_map/qkv/pallas_call | solution.py:726
  133.7 16.1 %attend.1 = (bf16[2048,128]{1,0:T(8,128)(2,1)}, f32[2048,128]{1,0:T(8,128)S(1)}, f32[2048,128]{1,0:T(8,128)S(1)}) custom-call(bf16[2,2048,128]{2,1,0:T(8,128)(2,1)S(1)} %get-tuple-element.38.q_ref, bf16[2,2048,128]{2,1,0:T(8,128)(2,1)S(1)} %get-tuple-element.39.k_ref, bf16[2,2048,128]{2,1,0:T(8,128)(2,1)S(1)} %get-tuple-element.40.v_ref), custom_call_target="tpu_custom_call" | custom-call | flops 8589934592 | bytes 4194304 | tf_op jit(solution)/shard_map/attend/pallas_call | solution.py:741
  151.8 3.5 all-to-all-start.1
  158.2 12.8 %all-to-all-done.1.o_ref = bf16[8,256,128]{2,1,0:T(8,128)(2,1)S(1)} async-done(((bf16[8,256,128]{2,1,0:T(8,128)(2,1)}), bf16[8,256,128]{2,1,0:T(8,128)(2,1)S(1)}, u32[]{:S(2)}, u32[]{:S(2)}) %all-to-all-start.1) | async-done | bytes 524320 | tf_op jit(solution)/shard_map/all_to_all | solution.py:756
  171.0 21.2 %all-gather.18.cloned.1.call-done = bf16[32,640,256]{2,1,0:T(8,128)(2,1)} async-done(((bf16[4,640,256]{2,1,0:T(8,128)(2,1)}), bf16[32,640,256]{2,1,0:T(8,128)(2,1)}) %all-gather.18.cloned.1.call-update) | async-done | bytes 10485776 | tf_op jit(solution)/shard_map/all_gather | solution.py:754
  192.1 14.4 %block.1 = (bf16[256,1024]{1,0:T(8,128)(2,1)}, f32[256,1024]{1,0:T(8,128)}, bf16[8,256,128]{2,1,0:T(8,128)(2,1)}, bf16[256,1024]{1,0:T(8,128)(2,1)}, bf16[256,20...) custom-call(s32[1]{0:T(128)} %bitcast.base_ref, ...), custom_call_target="tpu_custom_call" | custom-call | flops 5368709120 | bytes 16777216 | tf_op jit(solution)/shard_map/block/pallas_call | solution.py:759
  213.2 5.9 %weight_grads.1 = bf16[8,4,640,256]{3,2,1,0:T(8,128)(2,1)} custom-call(bf16[8,256,128]{2,1,0:T(8,128)(2,1)S(1)} %copy-done.7, bf16[256,1024]{1,0:T(8,128)(2,1)S(1)} %copy-done.13, bf16[256,1024]{1,0:T(8,128)(2,1)S(1)} %copy-done.11, bf16[256,2048]{1,0:T(8,128)(2,1)S(1)} %copy-done.8, bf16[256,2048]{1,0:T(8,128)(2,1)S(1)} %copy-done.9, ...), custom_call_target="tpu_custom_call" | custom-call | flops 2684354560 | bytes 16777216 | tf_op jit(solution)/shard_map/weight_grads/pallas_call | solution.py:776
  220.3 18.3 %all_to_all.26 = bf16[8,256,128]{2,1,0:T(8,128)(2,1)S(1)} all-to-all(bf16[8,256,128]{2,1,0:T(8,128)(2,1)S(1)} %copy-done.28), channel_id=1, replica_groups=mesh['grp'=4,'shard'=8] {'shard'}, dimensions={0} | all-to-all | bytes 1048576 | tf_op jit(solution)/shard_map/all_to_all | solution.py:773
  239.9 34.6 %attend_back.1 = (bf16[2048,128]{1,0:T(8,128)(2,1)S(1)}, bf16[2048,128]{1,0:T(8,128)(2,1)S(1)}, bf16[2048,128]{1,0:T(8,128)(2,1)S(1)}, f32[3,128]{1,0:T(4,128)S(1)}) custom-call(bf16[2,2048,128]{2,1,0:T(8,128)(2,1)S(1)} %copy-done.19, bf16[2,2048,128]{2,1,0:T(8,128)(2,1)S(1)} %copy-done.21, bf16[2,2048,128]{2,1,0:T(8,128)(2,1)S(1)} %copy-done.23, ...), custom_call_target="tpu_custom_call" | custom-call | flops 21474836480 | bytes 8388608 | tf_op jit(solution)/shard_map/attend_back/pallas_call | solution.py:794
  279.7 24.4 %all_to_all.27 = bf16[8,128,384]{1,2,0:T(8,128)(2,1)} all-to-all(bf16[8,128,384]{1,2,0:T(8,128)(2,1)S(1)} %copy.89), channel_id=1, replica_groups=mesh['grp'=4,'shard'=8] {'shard'}, dimensions={0} | all-to-all | bytes 1572864 | tf_op jit(solution)/shard_map/all_to_all | solution.py:823
  304.2 3.7 all-to-all-start.3
  311.9 3.3 collective-permute-start.6
  316.3 16.0 %all-to-all-done.3.d_ref = bf16[8,256,384]{2,1,0:T(8,128)(2,1)S(1)} async-done(((bf16[8,256,384]{2,1,0:T(8,128)(2,1)}), bf16[8,256,384]{2,1,0:T(8,128)(2,1)S(1)}, u32[]{:S(2)}, u32[]{:S(2)}) %all-to-all-start.3) | async-done | bytes 1572896 | tf_op jit(solution)/shard_map/all_to_all | solution.py:810
  336.4 4.9 %input_grad.1 = (f32[256,1024]{1,0:T(8,128)}, f32[8,1024]{1,0:T(8,128)S(1)}) custom-call(s32[1]{0:T(128)} %bitcast.base_ref, s32[8,9]{1,0:T(8,128)S(1)} %copy-done.15, bf16[8,256,384]{2,1,0:T(8,128)(2,1)S(1)} %all-to-all-done.3.d_ref, bf16[8,1024,384]{2,1,0:T(8,128)(2,1)S(1)} %copy-done.2, bf16[256,1024]{1,0:T(8,128)(2,1)S(1)} %copy-done.5, ...), custom_call_target="tpu_custom_call" | custom-call | flops 1610612736 | bytes 8388608 | tf_op jit(solution)/shard_map/input_grad/pallas_call | solution.py:812
  342.2 9.4 %all-gather.5 = f32[8,4,6144]{2,1,0:T(4,128)S(1)} all-gather(f32[1,4,6144]{2,1,0:T(4,128)S(1)} %maximum_bitcast_fusion.2), channel_id=5, replica_groups=mesh['grp'=4,'shard'=8] {'shard'}, dimensions={0}, use_global_device_ids=true | all-gather | bytes 884736 | tf_op jit(solution)/shard_map/all_gather | solution.py:831
  353.9 3.4 collective-permute-start
  362.4 11.0 %collective-permute-done.1 = f32[9,1536]{1,0:T(8,128)S(1)} collective-permute-done((f32[9,1536]{1,0:T(8,128)S(1)}, f32[9,1536]{1,0:T(8,128)S(1)}, u32[]{:S(2)}, u32[]{:S(2)}) %collective-permute-start.1) | collective-permute-done | bytes 55328 | tf_op jit(solution)/shard_map/ppermute | solution.py:662
  375.3 5.2 %collective-permute-start.4 = (f32[32,128]{1,0:T(8,128)S(1)}, f32[32,128]{1,0:T(8,128)S(1)}, u32[]{:S(2)}, u32[]{:S(2)}) collective-permute-start(f32[32,128]{1,0:T(8,128)S(1)} %fusion.16), channel_id=1, source_target_pairs={{0,16},{8,24},{16,0},{24,8},{1,17},{9,25},{17,1},{25,9},{2,18},{10... | collective-permute-start | bytes 49160 | tf_op jit(solution)/shard_map/ppermute | solution.py:662
  (218 shorter events, 68.7 us)
Async XLA Ops:
  7.2 38.4 %all-gather.16.cloned.1.call-start = ((), (), s32[]{:S(2)}) async-start(), calls=%async_computation.11 | async-start | bytes 1638400 | tf_op jit(solution)/shard_map/all_gather | solution.py:754
  9.9 73.5 %all-gather.20.cloned.1.call-start = ((), (), s32[]{:S(2)}) async-start(), calls=%async_computation.13 | async-start | bytes 2211840 | tf_op jit(solution)/shard_map/all_gather | solution.py:703
  14.1 31.6 %copy-start.30 = (bf16[128,768]{1,0:T(8,128)(2,1)S(1)}, bf16[128,768]{1,0:T(8,128)(2,1)}, u32[]{:S(2)}) copy-start(bf16[128,768]{1,0:T(8,128)(2,1)} %param.24) | copy-start | bytes 589828
  15.8 105.7 %all-gather.12.cloned.1.call-start = ((), (), s32[]{:S(2)}) async-start(), calls=%async_computation.7 | async-start | bytes 4718592 | tf_op jit(solution)/shard_map/all_gather | solution.py:688
  16.6 175.6 %all-gather.18.cloned.1.call-start = ((), (), s32[]{:S(2)}) async-start(), calls=%async_computation.12 | async-start | bytes 11796480 | tf_op jit(solution)/shard_map/all_gather | solution.py:754
  45.6 270.7 %all-gather.14.cloned.1.call-start = ((), (), s32[]{:S(2)}) async-start(), calls=%async_computation.8 | async-start | bytes 7077888 | tf_op jit(solution)/shard_map/all_gather | solution.py:811
  85.1 36.4 %copy-start.14 = (s32[8,9]{1,0:T(8,128)}, s32[8,9]{1,0:T(8,128)S(1)}, u32[]{:S(2)}) copy-start(s32[8,9]{1,0:T(8,128)S(1)} %slice_convert_fusion.seg_ref) | copy-start | bytes 868
  91.8 29.7 %copy-start.4 = (f32[2048,128]{1,0:T(8,128)}, f32[2048,128]{1,0:T(8,128)S(1)}, u32[]{:S(2)}) copy-start(f32[2048,128]{1,0:T(8,128)S(1)} %copy.86.cos_ref) | copy-start | bytes 3145732
  151.8 19.2 %all-to-all-start.1 = ((bf16[8,256,128]{2,1,0:T(8,128)(2,1)}), bf16[8,256,128]{2,1,0:T(8,128)(2,1)S(1)}, u32[]{:S(2)}, u32[]{:S(2)}) async-start(bf16[8,256,128]{2,1,0:T(8,128)(2,1)} %bitcast.11), calls=%async_computation.1 | async-start | bytes 1048576 | tf_op jit(solution)/shard_map/all_to_all | solution.py:756
  155.3 197.2 %reduce-scatter.3.cloned.1.call-start = ((), (), s32[]{:S(2)}) async-start(), calls=%async_computation.9 | async-start | bytes 11796480 | tf_op jit(solution)/shard_map/reduce_scatter | solution.py:788
  171.0 21.2 %copy-start.6 = (bf16[8,256,128]{2,1,0:T(8,128)(2,1)}, bf16[8,256,128]{2,1,0:T(8,128)(2,1)S(1)}, u32[]{:S(2)}) copy-start(bf16[8,256,128]{2,1,0:T(8,128)(2,1)S(1)} %all-to-all-done.1.o_ref) | copy-start | bytes 1572868
  239.9 35.0 %copy-start.17 = (bf16[2048,1024]{1,0:T(8,128)(2,1)S(1)}, bf16[2048,1024]{1,0:T(8,128)(2,1)}, u32[]{:S(2)}) copy-start(bf16[2048,1024]{1,0:T(8,128)(2,1)} %copy-done.16) | copy-start | bytes 12582916
  304.2 28.2 %all-to-all-start.3 = ((bf16[8,256,384]{2,1,0:T(8,128)(2,1)}), bf16[8,256,384]{2,1,0:T(8,128)(2,1)S(1)}, u32[]{:S(2)}, u32[]{:S(2)}) async-start(bf16[8,256,384]{2,1,0:T(8,128)(2,1)} %bitcast.112), calls=%async_computation.3 | async-start | bytes 3145728 | tf_op jit(solution)/shard_map/all_to_all | solution.py:810
  307.9 24.5 %copy-start.5 = (bf16[256,1024]{1,0:T(8,128)(2,1)S(1)}, bf16[256,1024]{1,0:T(8,128)(2,1)}, u32[]{:S(2)}) copy-start(bf16[256,1024]{1,0:T(8,128)(2,1)} %x_ref.3) | copy-start | bytes 1572868
  307.9 80.7 %reduce-scatter.5.cloned.1.call-start = ((), (), s32[]{:S(2)}) async-start(), calls=%async_computation.10 | async-start | bytes 1638400 | tf_op jit(solution)/shard_map/reduce_scatter | solution.py:789
  311.9 45.5 %collective-permute-start.6 = (bf16[128,768]{0,1:T(8,128)(2,1)}, bf16[128,768]{0,1:T(8,128)(2,1)}, u32[]{:S(2)}, u32[]{:S(2)}) collective-permute-start(bf16[128,768]{0,1:T(8,128)(2,1)} %get-tuple-element.143), channel_id=1, source_target_pairs={{0,24},{8,0},{16,8},{24,16},{1,25},{9,1},{17,9},{25,17},{2,26},{10... | collective-permute-start | bytes 589832 | tf_op jit(solution)/shard_map/ppermute | solution.py:662
  315.2 43.4 %collective-permute-start.7 = (bf16[128,768]{0,1:T(8,128)(2,1)}, bf16[128,768]{0,1:T(8,128)(2,1)}, u32[]{:S(2)}, u32[]{:S(2)}) collective-permute-start(bf16[128,768]{0,1:T(8,128)(2,1)} %get-tuple-element.145), channel_id=1, source_target_pairs={{0,16},{8,24},{16,0},{24,8},{1,17},{9,25},{17,1},{25,9},{2,18},{10... | collective-permute-start | bytes 589832 | tf_op jit(solution)/shard_map/ppermute | solution.py:662
  315.2 43.4 %collective-permute-start.8 = (bf16[128,768]{0,1:T(8,128)(2,1)}, bf16[128,768]{0,1:T(8,128)(2,1)}, u32[]{:S(2)}, u32[]{:S(2)}) collective-permute-start(bf16[128,768]{0,1:T(8,128)(2,1)} %get-tuple-element.144), channel_id=1, source_target_pairs={{0,8},{8,16},{16,24},{24,0},{1,9},{9,17},{17,25},{25,1},{2,10},{10... | collective-permute-start | bytes 589832 | tf_op jit(solution)/shard_map/ppermute | solution.py:662
  353.9 8.4 %collective-permute-start = (f32[9,1536]{1,0:T(8,128)S(1)}, f32[9,1536]{1,0:T(8,128)S(1)}, u32[]{:S(2)}, u32[]{:S(2)}) collective-permute-start(f32[9,1536]{1,0:T(8,128)S(1)} %bitcast.127), channel_id=1, source_target_pairs={{0,24},{8,0},{16,8},{24,16},{1,25},{9,1},{17,9},{25,17},{2,26},{10... | collective-permute-start | bytes 165896 | tf_op jit(solution)/shard_map/ppermute | solution.py:662
  357.4 16.1 %collective-permute-start.1 = (f32[9,1536]{1,0:T(8,128)S(1)}, f32[9,1536]{1,0:T(8,128)S(1)}, u32[]{:S(2)}, u32[]{:S(2)}) collective-permute-start(f32[9,1536]{1,0:T(8,128)S(1)} %bitcast.126), channel_id=1, source_target_pairs={{0,16},{8,24},{16,0},{24,8},{1,17},{9,25},{17,1},{25,9},{2,18},{10... | collective-permute-start | bytes 165896 | tf_op jit(solution)/shard_map/ppermute | solution.py:662
  357.5 16.0 %collective-permute-start.2 = (f32[9,1536]{1,0:T(8,128)S(1)}, f32[9,1536]{1,0:T(8,128)S(1)}, u32[]{:S(2)}, u32[]{:S(2)}) collective-permute-start(f32[9,1536]{1,0:T(8,128)S(1)} %bitcast.125), channel_id=1, source_target_pairs={{0,8},{8,16},{16,24},{24,0},{1,9},{9,17},{17,25},{25,1},{2,10},{10... | collective-permute-start | bytes 165896 | tf_op jit(solution)/shard_map/ppermute | solution.py:662
  375.2 11.6 %collective-permute-start.3 = (f32[32,128]{1,0:T(8,128)S(1)}, f32[32,128]{1,0:T(8,128)S(1)}, u32[]{:S(2)}, u32[]{:S(2)}) collective-permute-start(f32[32,128]{1,0:T(8,128)S(1)} %fusion.16), channel_id=1, source_target_pairs={{0,24},{8,0},{16,8},{24,16},{1,25},{9,1},{17,9},{25,17},{2,26},{10... | collective-permute-start | bytes 49160 | tf_op jit(solution)/shard_map/ppermute | solution.py:662
  375.3 11.6 %collective-permute-start.4 = (f32[32,128]{1,0:T(8,128)S(1)}, f32[32,128]{1,0:T(8,128)S(1)}, u32[]{:S(2)}, u32[]{:S(2)}) collective-permute-start(f32[32,128]{1,0:T(8,128)S(1)} %fusion.16), channel_id=1, source_target_pairs={{0,16},{8,24},{16,0},{24,8},{1,17},{9,25},{17,1},{25,9},{2,18},{10... | collective-permute-start | bytes 49160 | tf_op jit(solution)/shard_map/ppermute | solution.py:662
  380.5 6.3 %collective-permute-start.5 = (f32[32,128]{1,0:T(8,128)S(1)}, f32[32,128]{1,0:T(8,128)S(1)}, u32[]{:S(2)}, u32[]{:S(2)}) collective-permute-start(f32[32,128]{1,0:T(8,128)S(1)} %fusion.16), channel_id=1, source_target_pairs={{0,8},{8,16},{16,24},{24,0},{1,9},{9,17},{17,25},{25,1},{2,10},{10... | collective-permute-start | bytes 49160 | tf_op jit(solution)/shard_map/ppermute | solution.py:662
  (31 other events, 180.1 us)
Sparse Core Ops, SparseCore 0:
  10.2 35.3 all-gather.15
  48.1 29.4 all-gather.19
  79.4 42.0 all-gather.11
  123.2 68.8 all-gather.17
  194.4 51.1 all-gather.13
  249.0 98.9 reduce-scatter.2
  352.7 35.8 reduce-scatter.4

commit v2 on v1

--- a/solution.py
+++ b/solution.py
@@ -364,6 +364,9 @@
 
 
 LANES = 128
+FREE = pl.CostEstimate(flops=2**20, bytes_accessed=2**16, transcendentals=0)
+CHIPS = (2, 4, 6)
+ORDER = (0, 2, 4, 6, 1, 3, 5, 7)
 SEPARATE = -(2.0**100)
 GELU_C = 0.7978845608028654
 GELU_A = 0.044715
@@ -400,6 +403,11 @@
 def swap_halves(value):
     lane = lax.broadcasted_iota(jnp.int32, value.shape, 1)
     return jnp.where(lane % HD < HD // 2, pltpu.roll(value, 96, 1), pltpu.roll(value, 32, 1))
+
+
+def rotary(cos_ref, sin_ref, here):
+    cosine, sine = cos_ref[:, here].T, sin_ref[:, here].T
+    return jnp.concatenate([cosine] * 4, axis=1), jnp.concatenate([-sine, sine] * 2, axis=1)
 
 
 def members(seg_ref, block, rows):
@@ -425,18 +433,37 @@
     return [jnp.sum(column * value, axis=0, keepdims=True) for column in member]
 
 
-def qkv_kernel(seg_ref, x_ref, table_ref, w_ref, b_ref, cos_ref, sin_ref, q_ref, k_ref, v_ref, h_ref):
-    block = pl.program_id(0)
+def qkv_kernel(order_ref, seg_ref, *refs):
+    step = pl.program_id(0)
     last = pl.num_programs(0) - 1
-    rows = x_ref.shape[0]
+    *pieces, table_ref, w_ref, b_ref, cos_ref, sin_ref, q_ref, k_ref, v_ref, h_ref, x_all, arrived = refs
+    block = order_ref[step]
+    rows = x_all.shape[1]
+    copies, at = [], 0
+    for piece in pieces:
+        here = x_all.at[at : at + piece.shape[0]]
+        copies.append((at, pltpu.make_async_copy(piece, here, arrived.at[len(copies)])))
+        at += piece.shape[0]
+
+    @pl.when(step == 0)
+    def _():
+        for _, copy in copies:
+            copy.start()
+
+    for at, copy in copies:
+
+        @pl.when(step == at)
+        def _(copy=copy):
+            copy.wait()
+
     member = members(seg_ref, block, rows)
-    normal, _ = moments(x_ref[...].astype(f32))
+    normal, _ = moments(x_all[step].astype(f32))
     shift = mod_rows(table_ref, seg_ref, block, member, 0)
     scale = mod_rows(table_ref, seg_ref, block, member, 1)
     hidden = (normal * (1.0 + scale) + shift).astype(bf16)
     h_ref[...] = hidden
     projected = dot(hidden, w_ref[...]) + b_ref[...]
-    cosine, sine = cos_ref[...], sin_ref[...]
+    cosine, sine = rotary(cos_ref, sin_ref, slice(None))
     turned = []
     for part in range(2):
         piece = projected[:, part * LANES : (part + 1) * LANES]
@@ -489,23 +516,34 @@
 
 
 def block_kernel(
-    base_ref, seg_ref, x_ref, cot_ref, o_ref, table_ref, w_ref, b_out_ref, b_up_ref, b_down_ref,
-    out_ref, dx1_ref, do_ref, h2_ref, du_ref, act_ref, dff_ref, da_ref, slots_ref, gb_out_ref, gb_up_ref, gb_down_ref,
+    order_ref, seg_ref, x_ref, cot_ref, o_ref, table_ref, w_ref, b_out_ref, b_up_ref, b_down_ref,
+    out_ref, dx1_ref, do_ref, pair_ref, keep_ref, send_ref, slots_ref, gb_out_ref, gb_up_ref, gb_down_ref,
 ):
     rows = x_ref.shape[0]
-    shards, groups = w_ref.shape[:2]
-    block = base_ref[0]
+    groups, shards = w_ref.shape[:2]
+    block = order_ref[0]
     member = members(seg_ref, block, rows)
     modulation = partial(mod_rows, table_ref, seg_ref, block, member)
     wide = D // groups
 
     def weight(group, start):
-        return w_ref[:, group, start : start + LANES, :].reshape(D, wide)
+        return w_ref[group, :, start : start + LANES, :].reshape(D, wide)
 
     def weight_down(group):
-        return w_ref[:, group, 0 : 2 * LANES, :].reshape(2 * D, wide)
+        return w_ref[group, :, 0 : 2 * LANES, :].reshape(2 * D, wide)
+
+    def by_core(value, width, other):
+        parts = [value[:, at : at + width] for at in range(0, value.shape[1], width)]
+        even, odd = jnp.concatenate(parts[0::2], axis=1), jnp.concatenate(parts[1::2], axis=1)
+        return jnp.where((block % 2 == 0) != other, even, odd)
+
+    def share(start, value, width):
+        half = value.shape[1] // 2
+        keep_ref[:, start : start + half] = by_core(value, width, False)
+        send_ref[:, start : start + half] = by_core(value, width, True)
 
     mixed = jnp.concatenate([o_ref[shard] for shard in range(shards)], axis=1)
+    share(D, mixed, LANES)
     attn = jnp.concatenate([dot(mixed, weight(group, 256)) for group in range(groups)], axis=1)
     attn = attn + b_out_ref[...]
     gate1 = modulation(2)
@@ -513,12 +551,12 @@
     normal, inv = moments(after)
     scale2 = 1.0 + modulation(4)
     hidden = (normal * scale2 + modulation(3)).astype(bf16)
-    h2_ref[...] = hidden
+    share(D + D // 2, hidden, LANES)
     up = [dot(hidden, weight(group, start)) for group in range(groups) for start in (384, 512)]
     up = jnp.concatenate(up, axis=1) + b_up_ref[...]
     inner = jnp.tanh(GELU_C * (up + GELU_A * (up * up * up)))
     act = (0.5 * up * (1.0 + inner)).astype(bf16)
-    act_ref[...] = act
+    share(0, act, 2 * LANES)
     slope = 0.5 * (1.0 + inner) + (0.5 * GELU_C) * up * (1.0 - inner * inner) * (
         1.0 + (3.0 * GELU_A) * up * up
     )
@@ -529,17 +567,17 @@
 
     cot = cot_ref[...].astype(f32)
     dff = (gate2 * cot).astype(bf16)
-    dff_ref[...] = dff
+    pair_ref[:, 0:D] = dff
     gb_down_ref[...] = jnp.sum(dff.astype(f32), axis=0, keepdims=True)
     d_gate2 = slot_sums(member, cot * branch)
     d_act = sum(dot(dff[:, g * wide : (g + 1) * wide], weight_down(g), NT) for g in range(groups))
     du = (d_act * slope).astype(bf16)
-    du_ref[...] = du
+    pair_ref[:, 2 * D :] = du
     gb_up_ref[...] = jnp.sum(du.astype(f32), axis=0, keepdims=True)
     d_hidden = None
     for index in range(2 * groups):
         piece = du[:, index * wide : (index + 1) * wide]
-        term = dot(piece, weight(index // 2, 384 + 128 * (index % 2)), NT)
+        term = dot(piece, weight(index // 2, 384 + LANES * (index % 2)), NT)
         d_hidden = term if d_hidden is None else d_hidden + term
     d_shift2 = slot_sums(member, d_hidden)
     d_scale2 = slot_sums(member, d_hidden * normal)
@@ -547,7 +585,7 @@
     dx1_ref[...] = d_after
     d_gate1 = slot_sums(member, d_after * attn)
     da = (gate1 * d_after).astype(bf16)
-    da_ref[...] = da
+    pair_ref[:, D : 2 * D] = da
     gb_out_ref[...] = jnp.sum(da.astype(f32), axis=0, keepdims=True)
     d_mixed = sum(dot(da[:, g * wide : (g + 1) * wide], weight(g, 256), NT) for g in range(groups))
     d_mixed = d_mixed.astype(bf16)
@@ -556,21 +594,48 @@
     slots_ref[...] = jnp.concatenate(d_gate1 + d_shift2 + d_scale2 + d_gate2, axis=0)
 
 
-def weight_grad_kernel(o_ref, da_ref, h2_ref, du_ref, act_ref, dff_ref, g_ref):
-    shards = o_ref.shape[0]
-    wide = g_ref.shape[3]
-    g_ref[:, 0, 0:256, :] = dot(act_ref[...], dff_ref[...], TN).astype(bf16).reshape(shards, 256, wide)
-    mixed = jnp.concatenate([o_ref[shard] for shard in range(shards)], axis=1)
-    g_ref[:, 0, 256:384, :] = dot(mixed, da_ref[...], TN).astype(bf16).reshape(shards, LANES, wide)
-    for half in range(2):
-        piece = dot(h2_ref[...], du_ref[:, half * wide : (half + 1) * wide], TN).astype(bf16)
-        start = 384 + 128 * half
-        g_ref[:, 0, start : start + 128, :] = piece.reshape(shards, LANES, wide)
-
-
-def attend_back_kernel(
-    q_ref, k_ref, v_ref, do_ref, mixed_ref, l_ref, cos_ref, sin_ref, dq_ref, dk_ref, dv_ref, gb_ref, dn, dq_t
+def weight_grad_kernel(
+    order_ref, group_ref, keep_ref, send_ref, pair_ref, pair2_ref, first_x, first_y, own_x, own_y
 ):
+    groups, wide = 4, first_x.shape[3]
+
+    def product(at, width, start, stop):
+        here = pl.ds(pl.multiple_of(at, LANES), width)
+        return (
+            dot(keep_ref[:, here], pair_ref[:, start:stop], TN) + dot(send_ref[:, here], pair2_ref[:, start:stop], TN)
+        ).astype(bf16)
+
+    places = (((own_x, 0), (own_y, 0)), ((first_x, 0), (own_y, 1)), ((own_x, 1), (first_y, 0)), ((first_x, 1), (first_y, 1)))
+    for index in range(4):
+        chip = order_ref[index] // 2
+        down = product(chip * 2 * LANES, 2 * LANES, 0, D)
+        out = product(D + chip * LANES, LANES, D, 2 * D)
+        up = product(D + D // 2 + chip * LANES, LANES, 2 * D, 4 * D)
+        for group in range(groups):
+            to = (group + groups - group_ref[0]) % groups
+
+            def store(ref, entry, to):
+                ref[entry, to, 0:256, :] = down[:, group * wide : (group + 1) * wide]
+                ref[entry, to, 256:384, :] = out[:, group * wide : (group + 1) * wide]
+                for half in range(2):
+                    at = (2 * group + half) * wide
+                    ref[entry, to, 384 + 128 * half : 512 + 128 * half, :] = up[:, at : at + wide]
+
+            @pl.when(to < 2)
+            def _():
+                store(*places[index][0], to)
+
+            @pl.when(to >= 2)
+            def _():
+                store(*places[index][1], to - 2)
+
+
+def attend_back_kernel(head, q_ref, k_ref, v_ref, do_ref, mixed_ref, l_ref, cos_ref, sin_ref, *refs):
+    *refs, dn, dq_t, dk_all = refs
+    if head == 0:
+        qk_ref, dv_ref = refs
+    else:
+        qk_first, dv_first, qk_ref, own_ref, gb_ref = refs
     step = pl.program_id(0)
     rows = k_ref.shape[1]
     frames = q_ref.shape[1]
@@ -580,87 +645,125 @@
 
     @pl.when(step == 0)
     def _():
-        gb_ref[...] = jnp.zeros_like(gb_ref)
         dq_t[...] = jnp.zeros_like(dq_t)
         for at in range(0, frames, rows):
             here = slice(at, at + rows)
             d_out = do_ref[here].astype(f32)
             norm = l_ref[here]
             d_num = (d_out / norm).astype(bf16).astype(f32)
-            both = d_out * mixed_ref[here]
-            for head in range(2):
-                mine = low if head == 0 else ~low
-                total = jnp.sum(jnp.where(mine, both, 0.0), axis=1, keepdims=True)
-                delta = -total / norm[:, head * HD : head * HD + 1]
-                first = delta.astype(bf16).astype(f32)
-                second = (delta - first).astype(bf16).astype(f32)
-                third = delta - first - second
-                extra = jnp.where(lane == HD, first, jnp.where(lane == HD + 1, second, third))
-                extra = jnp.where(lane < HD + 3, extra, 0.0)
-                own = d_num if head == 0 else pltpu.roll(d_num, HD, 1)
-                dn[head, here] = jnp.where(low, own, extra).astype(bf16)
-
-    d_keys, d_values = [], []
-    for head in range(2):
-        key, value = k_ref[head], v_ref[head]
-        key_t = key.T
-        dk_total, dv_total = None, None
-        for at in range(0, frames, tile):
-            here = slice(at, at + tile)
-            query, d_num = q_ref[head, here], dn[head, here]
-            expo = jnp.exp(dot(key, query, NT))
-            d_score = (expo * dot(value, d_num, NT)).astype(bf16)
-            dk_term = dot(d_score, query)
-            dv_term = dot(expo.astype(bf16), d_num)
-            dk_total = dk_term if dk_total is None else dk_total + dk_term
-            dv_total = dv_term if dv_total is None else dv_total + dv_term
-            dq_t[head, :, here] += dot(key_t, d_score)
-        d_keys.append(dk_total)
-        d_values.append(dv_total)
-
-    def both_heads(pair):
-        return jnp.where(low, pair[0], pltpu.roll(pair[1], HD, 1))
-
-    def turn_back(value, here):
-        return (value * cos_ref[here] - swap_halves(value) * sin_ref[here]).astype(bf16)
+            mine = low if head == 0 else ~low
+            total = jnp.sum(jnp.where(mine, d_out * mixed_ref[here], 0.0), axis=1, keepdims=True)
+            delta = -total / norm[:, head * HD : head * HD + 1]
+            first = delta.astype(bf16).astype(f32)
+            second = (delta - first).astype(bf16).astype(f32)
+            third = delta - first - second
+            extra = jnp.where(lane == HD, first, jnp.where(lane == HD + 1, second, third))
+            extra = jnp.where(lane < HD + 3, extra, 0.0)
+            own = d_num if head == 0 else pltpu.roll(d_num, HD, 1)
+            dn[here] = jnp.where(low, own, extra).astype(bf16)
+
+    key, value = k_ref[0], v_ref[0]
+    key_t = key.T
+    dk_total, dv_total = None, None
+    for at in range(0, frames, tile):
+        here = slice(at, at + tile)
+        query, d_num = q_ref[0, here], dn[here]
+        expo = jnp.exp(dot(key, query, NT))
+        d_score = (expo * dot(value, d_num, NT)).astype(bf16)
+        dk_term = dot(d_score, query)
+        dv_term = dot(expo.astype(bf16), d_num)
+        dk_total = dk_term if dk_total is None else dk_total + dk_term
+        dv_total = dv_term if dv_total is None else dv_total + dv_term
+        dq_t[:, here] += dot(key_t, d_score)
 
     here = pl.ds(pl.multiple_of(step * rows, rows), rows)
-    d_key = turn_back(both_heads(d_keys), here)
-    d_value = both_heads(d_values).astype(bf16)
-    dk_ref[...] = d_key
-    dv_ref[...] = d_value
-    gb_ref[1:2] += jnp.sum(d_key.astype(f32), axis=0, keepdims=True)
-    gb_ref[2:3] += jnp.sum(d_value.astype(f32), axis=0, keepdims=True)
+    dk_all[here] = dk_total
+    if head == 0:
+        dv_ref[here] = dv_total.astype(bf16)
+    else:
+        own_ref[here, 2 * LANES :] = jnp.where(low, dv_first[here].astype(f32), pltpu.roll(dv_total, HD, 1)).astype(bf16)
 
     @pl.when(step == pl.num_programs(0) - 1)
     def _():
         for at in range(0, frames, rows):
             part = slice(at, at + rows)
-            d_query = both_heads([0.125 * dq_t[head, :, part].T for head in range(2)])
-            d_query = turn_back(d_query, part)
-            dq_ref[part] = d_query
-            gb_ref[0:1] += jnp.sum(d_query.astype(f32), axis=0, keepdims=True)
-
-
-def input_grad_kernel(base_ref, seg_ref, d_ref, w_ref, x_ref, dx1_ref, table_ref, grad_ref, slots_ref):
+            cosine, sine = rotary(cos_ref, sin_ref, part)
+            both = jnp.where(low, 0.125 * dq_t[:, part].T, pltpu.roll(dk_all[part], HD, 1))
+            both = (both * cosine - swap_halves(both) * sine).astype(bf16)
+            qk_ref[part] = both
+            if head == 1:
+                first, second = qk_first[part].astype(f32), both.astype(f32)
+                own_ref[part, 0:LANES] = jnp.where(low, first, pltpu.roll(second, HD, 1)).astype(bf16)
+                own_ref[part, LANES : 2 * LANES] = jnp.where(low, pltpu.roll(first, HD, 1), second).astype(bf16)
+        if head == 1:
+            ones = jnp.ones((8, frames), bf16)
+            sums = dot(ones, own_ref[...])[0:1]
+            for index in range(3):
+                gb_ref[index : index + 1] = sums[:, index * LANES : (index + 1) * LANES]
+
+
+def input_grad_kernel(
+    base_ref, seg_ref, first_ref, second_ref, w_ref, x_ref, dx1_ref, table_ref, grad_ref, slots_ref
+):
     block = base_ref[0]
     rows = x_ref.shape[0]
     member = members(seg_ref, block, rows)
     scale = 1.0 + mod_rows(table_ref, seg_ref, block, member, 1)
-    d_hidden = sum(dot(d_ref[shard], w_ref[shard], NT) for shard in range(d_ref.shape[0]))
+    low = lax.broadcasted_iota(jnp.int32, (rows, LANES), 1) < HD
+    d_hidden = None
+    for shard in range(first_ref.shape[0]):
+        first, second = first_ref[shard].astype(f32), second_ref[shard, :, :LANES].astype(f32)
+        queries = jnp.where(low, first, pltpu.roll(second, HD, 1)).astype(bf16)
+        keys = jnp.where(low, pltpu.roll(first, HD, 1), second).astype(bf16)
+        whole_row = jnp.concatenate([queries, keys, second_ref[shard, :, LANES:]], axis=1)
+        term = dot(whole_row, w_ref[shard], NT)
+        d_hidden = term if d_hidden is None else d_hidden + term
     normal, inv = moments(x_ref[...].astype(f32))
     grad_ref[...] = dx1_ref[...] + norm_back(d_hidden * scale, normal, inv)
     sums = slot_sums(member, d_hidden) + slot_sums(member, d_hidden * normal)
     slots_ref[...] = jnp.concatenate(sums + [jnp.zeros((2, D), f32)], axis=0)
 
 
-def exchange(pieces, axis, size):
+def spread(value, axis, size):
+    return [value] + [
+        lax.ppermute(value, axis, [(i, (i - step) % size) for i in range(size)]) for step in range(1, size)
+    ]
+
+
+def trade(pieces, axis, size):
+    return [pieces[0]] + [
+        lax.ppermute(pieces[size - step], axis, [(i, (i - step) % size) for i in range(size)])
+        for step in range(1, size)
+    ]
+
+
+def in_order(pieces, axis, size):
     own = lax.axis_index(axis)
-    out = [lax.dynamic_index_in_dim(pieces, own, 0, keepdims=False)]
-    for step in range(1, size):
-        block = lax.dynamic_index_in_dim(pieces, (own - step) % size, 0, keepdims=False)
-        out.append(lax.ppermute(block, axis, [(i, (i - step) % size) for i in range(size)]))
+    out = []
+    for place in range(size):
+        pick = (place - own) % size
+        value = pieces[0]
+        for index in range(1, size):
+            value = jnp.where(pick == index, pieces[index], value)
+        out.append(value)
     return out
+
+
+def hop(value, step):
+    return lax.ppermute(value, "shard", [(i, i ^ step) for i in range(8)])
+
+
+def after(value, *others):
+    anywhere = pl.BlockSpec(memory_space=pl.ANY)
+    return pl.pallas_call(
+        lambda *refs: None,
+        in_specs=[anywhere] * (1 + len(others)),
+        out_specs=anywhere,
+        out_shape=jax.ShapeDtypeStruct(value.shape, value.dtype),
+        input_output_aliases={0: 0},
+        cost_estimate=FREE,
+        name="after",
+    )(value, *others)
 
 
 def shape(*dims, kind=bf16):
@@ -685,57 +788,80 @@
     depth = D // shards
     wide = D // groups
 
-    frames_all = lax.all_gather(frames, "shard", axis=0, tiled=True)
-    w_cols = lax.all_gather(w_qkv, "grp", axis=1, tiled=True)
-    w_cols = w_cols.reshape(depth, 3, shards, LANES).transpose(2, 0, 1, 3).reshape(shards, depth, 3 * LANES)
-    w_heads = lax.all_to_all(w_cols, "shard", split_axis=0, concat_axis=0, tiled=True).reshape(D, 3 * LANES)
+    group = lax.axis_index("grp")
+    order = shard ^ jnp.array(ORDER, jnp.int32)
+
+    inverse = 10000.0 ** (-jnp.arange(HD // 2, dtype=f32) / (HD // 2))
+    phase = inverse[:, None] * jnp.arange(packed, dtype=f32)[None, :]
+    cosine, sine = jnp.cos(phase), jnp.sin(phase)
 
     activated = jax.nn.silu(time_table).astype(bf16)
     act_own = lax.dynamic_slice_in_dim(activated, shard * depth, depth, 1)
     partial_mod = dot(act_own, w_ada)
     mod_wide = partial_mod.shape[1]
-    segs = jnp.concatenate((seg_start, seg_length, seg_step), axis=1).astype(f32)
     biases = [b.astype(f32) for b in (b_ada, b_qkv, b_out, b_up, b_down)]
     sizes = [b.shape[0] for b in biases]
-    extra = jnp.concatenate(biases + [segs[0]])
+    segs = jnp.concatenate((seg_start, seg_length, seg_step), axis=1).astype(f32)
+    extra = jnp.concatenate(biases + [jnp.floor(segs[0] / 128.0), segs[0] % 128.0])
     extra_rows = -(-extra.shape[0] // mod_wide)
     extra = jnp.pad(extra, (0, extra_rows * mod_wide - extra.shape[0])).reshape(extra_rows, mod_wide)
-    small = lax.all_gather(jnp.concatenate((partial_mod, extra), axis=0), "shard", axis=0)
-    mod_own = jnp.sum(small[:, :steps], axis=0)
+    units = 3 * shards // groups
+    first = group * units
+    by_unit = w_qkv.reshape(depth, units, LANES).transpose(1, 0, 2)
+    which = jnp.minimum((jnp.arange(shards) - first) % shards, units - 1)
+    by_shard = jnp.take(by_unit, which, axis=0, mode="clip")
+    w_cols = jnp.broadcast_to(by_shard[None], (groups, shards, depth, LANES)).reshape(groups * shards, depth, LANES)
+    w_cols = lax.all_to_all(w_cols, ("grp", "shard"), split_axis=0, concat_axis=0, tiled=True).reshape(groups, D, LANES)
+    small = jnp.concatenate((partial_mod, extra), axis=0).astype(bf16)
+    small = lax.all_gather(small, "shard", axis=0).astype(f32)
+    held = after(frames, small)
+    chips = [held] + [hop(held, step) for step in CHIPS]
+
+    mod_own = jnp.sum(small[:, :steps], axis=0).astype(bf16)
+    high = lax.all_gather(after(mod_own, w_cols), "grp", axis=1, tiled=True)
+
+    w_heads = jnp.concatenate(
+        [lax.dynamic_index_in_dim(w_cols, (part * shards + shard) // units, 0, keepdims=False) for part in range(3)], axis=1
+    )
+
+    chips = [chips[0]] + [after(piece, high) for piece in chips[1:]]
+    others = hop(jnp.stack(chips), 1)
+
+    pack = jnp.concatenate((w_down, w_out, w_up[:, :wide], w_up[:, wide:]), axis=0)
+    weights = lax.all_gather(pack, ("grp", "shard"), axis=0).reshape(groups, shards, 5 * LANES, wide)
+
     extra = small[:, steps:].reshape(shards, extra_rows * mod_wide)
     full, at = [], 0
     for size in sizes:
         full.append(extra[:, at : at + size].reshape(1, shards * size))
         at += size
     ada_bias, qkv_bias, out_bias, up_bias, down_bias = full
-    seg_all = extra[:, at : at + 9].astype(jnp.int32)
-    table = lax.all_gather(mod_own, "grp", axis=1, tiled=True) + ada_bias
+    seg_all = (extra[:, at : at + 9] * 128.0 + extra[:, at + 9 : at + 18]).astype(jnp.int32)
     qkv_bias = lax.dynamic_index_in_dim(qkv_bias.reshape(3, shards, LANES), shard, 1, keepdims=False)
     qkv_bias = qkv_bias.reshape(1, 3 * LANES)
-
-    place = jnp.arange(packed, dtype=jnp.int32).reshape(shards, rows)
-    begin = seg_all[:, None, 0:3]
-    inside = (place[:, :, None] >= begin) & (place[:, :, None] < begin + seg_all[:, None, 3:6])
-    seg_low = jnp.sum(jnp.where(inside, begin, 0), axis=2)
-    cosine, sine = angles((place - seg_low).astype(f32).reshape(packed))
-    cosine = jnp.tile(cosine, (1, 4))
-    sine = jnp.concatenate((-sine, sine, -sine, sine), axis=1)
-
+    table = high.astype(f32) + ada_bias
+
+    ordered = lambda width: pl.BlockSpec((rows, width), lambda i, order: (order[i], 0))
+    ordered_heads = pl.BlockSpec((2, rows, LANES), lambda i, order: (0, order[i], 0))
     by_block = lambda width: pl.BlockSpec((rows, width), lambda i: (i, 0))
     two_heads = pl.BlockSpec((2, rows, LANES), lambda i: (0, i, 0))
+    frame_pieces = [piece[None] for piece in chips] + [others]
     q, k, v, h1_all = pl.pallas_call(
         qkv_kernel,
-        grid=(shards,),
-        in_specs=[
-            smem, by_block(D), whole(steps, 2 * D), whole(D, 3 * LANES), whole(1, 3 * LANES),
-            by_block(LANES), by_block(LANES),
-        ],
-        out_specs=[two_heads, two_heads, two_heads, by_block(D)],
+        grid_spec=pltpu.PrefetchScalarGridSpec(
+            num_scalar_prefetch=1,
+            grid=(shards,),
+            in_specs=[smem]
+            + [pl.BlockSpec(memory_space=pl.ANY)] * len(frame_pieces)
+            + [whole(steps, 2 * D), whole(D, 3 * LANES), whole(1, 3 * LANES)] + [pl.BlockSpec((HD // 2, rows), lambda i, order: (0, order[i]))] * 2,
+            out_specs=[ordered_heads] * 3 + [ordered(D)],
+            scratch_shapes=[pltpu.VMEM((shards, rows, D), bf16), pltpu.SemaphoreType.DMA((len(frame_pieces),))],
+        ),
         out_shape=[shape(2, packed, LANES)] * 3 + [shape(packed, D)],
-        compiler_params=params(40),
-        cost_estimate=pl.CostEstimate(flops=2 * packed * D * 384, bytes_accessed=2 * packed * D * 4, transcendentals=0),
+        compiler_params=params(60),
+        cost_estimate=FREE,
         name="qkv",
-    )(seg_all, frames_all, table[:, : 2 * D], w_heads, qkv_bias, cosine, sine)
+    )(order, seg_all, *frame_pieces, table[:, : 2 * D], w_heads, qkv_bias, cosine, sine)
 
     attn_flops = 2 * 2 * packed * packed * 256
     o_heads, mixed, norm = pl.pallas_call(
@@ -744,91 +870,125 @@
         in_specs=[two_heads, whole(2, packed, LANES), whole(2, packed, LANES)],
         out_specs=[by_block(LANES)] * 3,
         out_shape=[shape(packed, LANES), shape(packed, LANES, kind=f32), shape(packed, LANES, kind=f32)],
-        compiler_params=params(40),
-        cost_estimate=pl.CostEstimate(flops=2 * attn_flops, bytes_accessed=2**22, transcendentals=2 * packed * packed),
+        compiler_params=params(60),
+        cost_estimate=FREE,
         name="attend",
     )(q, k, v)
-
-    pack = jnp.concatenate((w_down, w_out, w_up[:, :wide], w_up[:, wide:]), axis=0)
-    pack_rows = pack.shape[0]
-    weights = lax.all_gather(lax.all_gather(pack, "grp", axis=0), "shard", axis=0)
 
     o = lax.all_to_all(o_heads.reshape(shards, rows, LANES), "shard", split_axis=0, concat_axis=0, tiled=True)
     base = shard.astype(jnp.int32).reshape(1)
     block_flops = 2 * rows * D * D * 10
-    out, dx1, d_mixed, h2, du, act, dff, da, slots_ff, gb_out, gb_up, gb_down = pl.pallas_call(
+    out, dx1, d_mixed, pair, keep, send, slots_ff, gb_out, gb_up, gb_down = pl.pallas_call(
         block_kernel,
-        in_specs=[smem, smem] + [pl.BlockSpec(memory_space=pltpu.VMEM)] * 8,
-        out_specs=[pl.BlockSpec(memory_space=pltpu.VMEM)] * 12,
+        grid=(1,),
+        in_specs=[
+            smem, smem, whole(rows, D), whole(rows, D), whole(shards, rows, LANES), whole(steps, 6 * D),
+            whole(groups, shards, 5 * LANES, wide), whole(1, D), whole(1, 2 * D), whole(1, D),
+        ],
+        out_specs=[
+            whole(rows, D), whole(rows, D), whole(shards, rows, LANES), whole(rows, 4 * D), whole(rows, 2 * D),
+            whole(rows, 2 * D), whole(12, D), whole(1, D), whole(1, 2 * D), whole(1, D),
+        ],
         out_shape=[
-            shape(rows, D), shape(rows, D, kind=f32), shape(shards, rows, LANES), shape(rows, D), shape(rows, 2 * D),
-            shape(rows, 2 * D), shape(rows, D), shape(rows, D), shape(12, D, kind=f32),
+            shape(rows, D), shape(rows, D, kind=f32), shape(shards, rows, LANES), shape(rows, 4 * D), shape(rows, 2 * D),
+            shape(rows, 2 * D), shape(12, D, kind=f32),
             shape(1, D, kind=f32), shape(1, 2 * D, kind=f32), shape(1, D, kind=f32),
         ],
-        compiler_params=pltpu.CompilerParams(vmem_limit_bytes=56 * 2**20),
-        cost_estimate=pl.CostEstimate(flops=block_flops, bytes_accessed=2**24, transcendentals=rows * 2 * D),
+        compiler_params=params(60),
+        cost_estimate=FREE,
         name="block",
-    )(base, seg_all, frames, cotangent, o, table, weights, out_bias, up_bias, down_bias)
+    )(order, seg_all, frames, cotangent, o, table, weights, out_bias, up_bias, down_bias)
 
     d_heads = lax.all_to_all(d_mixed, "shard", split_axis=0, concat_axis=0, tiled=True).reshape(packed, LANES)
 
-    by_group = lambda width: pl.BlockSpec((rows, width), lambda i: (0, i))
-    grad_pack = pl.pallas_call(
+    send, pair_send = hop(send, 1), hop(pair, 1)
+    half = (2, groups // 2, 5 * LANES, wide)
+    first_x, first_y, own_x, own_y = pl.pallas_call(
         weight_grad_kernel,
-        grid=(groups,),
-        in_specs=[
-            whole(shards, rows, LANES), by_group(wide), whole(rows, D), by_group(2 * wide), whole(rows, 2 * D), by_group(wide),
-        ],
-        out_specs=pl.BlockSpec((shards, 1, pack_rows, wide), lambda i: (0, i, 0, 0)),
-        out_shape=shape(shards, groups, pack_rows, wide),
-        compiler_params=params(40),
-        cost_estimate=pl.CostEstimate(flops=block_flops // 2, bytes_accessed=2**24, transcendentals=0),
+        grid=(1,),
+        in_specs=[smem, smem, whole(rows, 2 * D), whole(rows, 2 * D), whole(rows, 4 * D), whole(rows, 4 * D)],
+        out_specs=[whole(*half)] * 4,
+        out_shape=[shape(*half)] * 4,
+        compiler_params=params(60),
+        cost_estimate=FREE,
         name="weight_grads",
-    )(o, da, h2, du, act, dff)
-    grad_pack = lax.psum_scatter(grad_pack, "shard", scatter_dimension=0, tiled=False)
-    grad_pack = lax.psum_scatter(grad_pack, "grp", scatter_dimension=0, tiled=False).astype(f32)
-    g_down = grad_pack[: 2 * LANES]
-    g_out = grad_pack[2 * LANES : 3 * LANES]
-    g_up = jnp.concatenate((grad_pack[3 * LANES : 4 * LANES], grad_pack[4 * LANES :]), axis=1)
-
-    dq, dk, dv, gb_qkv = pl.pallas_call(
-        attend_back_kernel,
+    )(order, group.astype(jnp.int32).reshape(1), keep, send, pair, pair_send)
+    first_x, first_y = after(first_x, d_heads), after(first_y, d_heads)
+    d_heads = after(d_heads, first_x, first_y)
+    add = lambda *pieces: sum(piece.astype(f32) for piece in pieces).astype(bf16)
+
+    back_specs = lambda head: [
+        pl.BlockSpec((1, packed, LANES), lambda i: (head, 0, 0)),
+        pl.BlockSpec((1, rows, LANES), lambda i: (head, i, 0)),
+        pl.BlockSpec((1, rows, LANES), lambda i: (head, i, 0)),
+    ] + [whole(packed, LANES)] * 3 + [whole(HD // 2, packed)] * 2
+    back_scratch = [pltpu.VMEM((packed, LANES), bf16), pltpu.VMEM((LANES, packed), f32), pltpu.VMEM((packed, LANES), f32)]
+    arguments = (q, k, v, d_heads, mixed, norm, cosine, sine)
+    came_x, came_y = hop(first_x, 2), hop(first_y, 4)
+    qk_first, dv_first = pl.pallas_call(
+        partial(attend_back_kernel, 0),
         grid=(shards,),
-        in_specs=[
-            whole(2, packed, LANES), two_heads, two_heads, whole(packed, LANES), whole(packed, LANES),
-            whole(packed, LANES), whole(packed, LANES), whole(packed, LANES),
-        ],
-        out_specs=[whole(packed, LANES), by_block(LANES), by_block(LANES), whole(3, LANES)],
-        out_shape=[shape(packed, LANES)] * 3 + [shape(3, LANES, kind=f32)],
-        scratch_shapes=[pltpu.VMEM((2, packed, LANES), bf16), pltpu.VMEM((2, LANES, packed), f32)],
-        compiler_params=params(48),
-        cost_estimate=pl.CostEstimate(flops=5 * attn_flops, bytes_accessed=2**23, transcendentals=2 * packed * packed),
-        name="attend_back",
-    )(q, k, v, d_heads, mixed, norm, cosine, sine)
-
-    d_own = jnp.concatenate((dq, dk, dv), axis=1)
-    d_rows = lax.all_to_all(d_own.reshape(shards, rows, 3 * LANES), "shard", split_axis=0, concat_axis=0, tiled=True)
-    w_all = lax.all_gather(w_heads, "shard", axis=0)
+        in_specs=back_specs(0),
+        out_specs=[whole(packed, LANES), whole(packed, LANES)],
+        out_shape=[shape(packed, LANES)] * 2,
+        scratch_shapes=back_scratch,
+        compiler_params=params(60),
+        cost_estimate=FREE,
+        name="attend_back_first",
+    )(*arguments)
+    came_x, came_y = after(came_x, qk_first), after(came_y, qk_first)
+    next_y, next_x = add(own_x[1], came_x[1]), add(own_y[1], came_y[1])
+    dv_first = after(dv_first, next_y, next_x)
+    next_y, next_x = hop(next_y, 4), hop(next_x, 2)
+    d_first = lax.all_to_all(qk_first.reshape(shards, rows, LANES), "shard", split_axis=0, concat_axis=0, tiled=True)
+    qk_second, d_own, gb_qkv = pl.pallas_call(
+        partial(attend_back_kernel, 1),
+        grid=(shards,),
+        in_specs=back_specs(1) + [whole(packed, LANES)] * 2,
+        out_specs=[whole(packed, LANES), whole(packed, 3 * LANES), whole(3, LANES)],
+        out_shape=[shape(packed, LANES), shape(packed, 3 * LANES), shape(3, LANES, kind=f32)],
+        scratch_shapes=back_scratch,
+        compiler_params=params(60),
+        cost_estimate=FREE,
+        name="attend_back_second",
+    )(*arguments, qk_first, dv_first)
+    next_y, next_x = after(next_y, qk_second), after(next_x, qk_second)
+    totals = (add(own_x[0], came_x[0], next_y), add(own_y[0], came_y[0], next_x))
+    d_own_late = after(d_own, *totals)
+    grads = trade([totals[i // 2][i % 2] for i in range(groups)], "grp", groups)
+    grads = sum(piece.astype(f32) for piece in grads)
+    g_down, g_out = grads[: 2 * LANES], grads[2 * LANES : 3 * LANES]
+    g_up = jnp.concatenate((grads[3 * LANES : 4 * LANES], grads[4 * LANES :]), axis=1)
+
+    second = jnp.concatenate((qk_second.reshape(shards, rows, LANES), d_own[:, 2 * LANES :].reshape(shards, rows, LANES)), axis=2)
+    d_second = lax.all_to_all(second, "shard", split_axis=0, concat_axis=0, tiled=True)
+    w_all = lax.all_gather(after(w_heads, o), "shard", axis=0)
     grad_frames, slots_qkv = pl.pallas_call(
         input_grad_kernel,
-        in_specs=[smem, smem] + [pl.BlockSpec(memory_space=pltpu.VMEM)] * 5,
+        in_specs=[smem, smem] + [pl.BlockSpec(memory_space=pltpu.VMEM)] * 6,
         out_specs=[pl.BlockSpec(memory_space=pltpu.VMEM)] * 2,
         out_shape=[shape(rows, D, kind=f32), shape(8, D, kind=f32)],
         compiler_params=pltpu.CompilerParams(vmem_limit_bytes=40 * 2**20),
-        cost_estimate=pl.CostEstimate(flops=2 * rows * D * 3 * D, bytes_accessed=2**23, transcendentals=0),
+        cost_estimate=FREE,
         name="input_grad",
-    )(base, seg_all, d_rows, w_all, frames, dx1, table[:, : 2 * D])
-
-    g_heads = dot(h1_all, d_own, TN).astype(bf16).reshape(shards, depth, 3 * LANES)
-    g_rows = lax.all_to_all(g_heads, "shard", split_axis=0, concat_axis=0, tiled=True)
-    g_rows = g_rows.reshape(shards, depth, 3, LANES).transpose(1, 2, 0, 3).reshape(depth, groups, 3 * D // groups)
-    g_qkv = sum(piece.astype(f32) for piece in exchange(g_rows.transpose(1, 0, 2), "grp", groups))
+    )(base, seg_all, d_first, d_second, w_all, frames, dx1, table[:, : 2 * D])
+
+    g_heads = dot(h1_all, d_own_late, TN).astype(bf16).reshape(shards, depth, 3 * LANES)
+    part = jnp.stack([jnp.clip((units * to + units - 1 - shard) // shards, 0, 2) for to in range(groups)])
+    g_send = jnp.stack(
+        [lax.dynamic_slice_in_dim(g_heads, part[to] * LANES, LANES, 2) for to in range(groups)]
+    ).reshape(groups * shards, depth, LANES)
+    g_came = lax.all_to_all(g_send, ("grp", "shard"), split_axis=0, concat_axis=0, tiled=True)
+    g_came = jnp.sum(g_came.reshape(groups, shards, depth, LANES).astype(f32), axis=0)
+    g_qkv = jnp.concatenate(
+        [lax.dynamic_index_in_dim(g_came, (first + unit) % shards, 0, keepdims=False) for unit in range(units)], axis=1
+    )
 
     d_slot = jnp.concatenate((slots_qkv[:6], slots_ff), axis=0).reshape(6, 3, D).transpose(1, 0, 2).reshape(3, 6 * D)
     row_sums = jnp.concatenate((gb_qkv.reshape(-1), gb_out[0], gb_up[0], gb_down[0]))
     sum_rows = -(-row_sums.shape[0] // (6 * D))
     row_sums = jnp.pad(row_sums, (0, sum_rows * 6 * D - row_sums.shape[0])).reshape(sum_rows, 6 * D)
-    tail = lax.all_gather(jnp.concatenate((d_slot, row_sums), axis=0), "shard", axis=0)
+    tail = lax.all_gather(after(jnp.concatenate((d_slot, row_sums), axis=0), grads), "shard", axis=0)
     d_slots = tail[:, :3]
     d_segs = jnp.concatenate(
         (d_slots[0], d_slots[shards - 1], jnp.sum(d_slots[1 : shards - 1], axis=(0, 1))[None]), axis=0
@@ -843,11 +1003,10 @@
     own_sums = [lax.dynamic_slice_in_dim(total, shard * size, size) for total, size in zip(sums, sizes)]
     send = jnp.concatenate(own_sums + [step_ids])
     send_rows = -(-send.shape[0] // mod_wide)
-    send = jnp.pad(send, (0, send_rows * mod_wide - send.shape[0])).reshape(1, send_rows, mod_wide)
-    parts = jnp.concatenate(
-        (d_segs.reshape(7, groups, mod_wide).transpose(1, 0, 2), jnp.broadcast_to(send, (groups, send_rows, mod_wide))), axis=1
-    )
-    parts = exchange(parts, "grp", groups)
+    send = jnp.pad(send, (0, send_rows * mod_wide - send.shape[0])).reshape(send_rows, mod_wide)
+    d_segs = d_segs.reshape(7, groups, mod_wide).transpose(1, 0, 2)
+    at_group = lambda pieces: [lax.dynamic_index_in_dim(pieces, (group + i) % groups, 0, keepdims=False) for i in range(groups)]
+    parts = trade([jnp.concatenate((piece, send), axis=0) for piece in at_group(d_segs)], "grp", groups)
     d_rows_all = jnp.concatenate([piece[:7] for piece in parts], axis=0)
     rest = [piece[7:].reshape(-1) for piece in parts]
     at = sum(sizes)
@@ -865,8 +1024,7 @@
     d_act = lax.dot_general(d_table, w_ada.astype(f32), NT, precision=top_precision, preferred_element_type=f32)
     table_own = lax.dynamic_slice_in_dim(time_table, shard * depth, depth, 1)
     g_table = jax.vjp(jax.nn.silu, table_own)[1](d_act)[0]
-    for_all = jnp.broadcast_to(g_table[None], (groups,) + g_table.shape)
-    g_table = sum(exchange(for_all, "grp", groups))
+    g_table = sum(spread(g_table, "grp", groups))
     return (
         out, grad_frames, g_table, g_ada, gb_ada, g_qkv, gb_qkv, g_out, gb_out, g_up, gb_up, g_down, gb_down,
     )

time: 400 us -> 353 us (0.88); the launches traced: 399 us -> 346 us
  waiting for transfers between devices: 97.8 us -> 45 us
  blocking collectives: 108 us -> 61.8 us
  Pallas kernels: 88.2 us -> 111 us
  starting transfers between devices: 24 us -> 42.5 us
  other arithmetic: 25.1 us -> 30.3 us
    all_gather x5 -> x2, waiting for transfers between devices: 54.4 us -> 0.02 us  [the longest x1 0.02 us: local_heads(): w_all = lax.all_gather(after(w_heads, o), 'shard', axis=0)]
    all_to_all x3 -> x1, blocking collectives: 60.9 us -> 14.2 us  [local_heads(): lax.all_to_all(o_heads.reshape(shards, rows, LANES), 'shard', split_axis=...]
    pallas_call x4 -> x21, Pallas kernels: 67.2 us -> 88.4 us  [the longest x1 24.3 us: local_heads(): pl.pallas_call(partial(attend_back_kernel, 1), grid=(shards,), in_specs=b...]
    ppermute x9 -> x19, waiting for transfers between devices: 12.7 us -> 30 us  [the longest x10 23.2 us: hop(): return lax.ppermute(value, 'shard', [(i, i ^ step) for i in range(8)])]
    all_to_all x2 -> x5, starting transfers between devices: 7.25 us -> 21.6 us  [the longest x1 7.3 us: local_heads(): lax.all_to_all(w_cols, ('grp', 'shard'), split_axis=0, concat_axis=0, til...]
    all_to_all x2 -> x5, waiting for transfers between devices: 28.8 us -> 15 us  [the longest x1 8.09 us: local_heads(): lax.all_to_all(second, 'shard', split_axis=0, concat_axis=0, tiled=True)]
    convert_element_type x2 -> x6, other arithmetic: 1.02 us -> 10 us  [the longest x4 7.73 us: local_heads(): sum((piece.astype(f32) for piece in pieces)).astype(bf16)]
    neg x1 -> x0, other arithmetic: 5.54 us -> none  [local_heads(): sine = jnp.concatenate((-sine, sine, -sine, sine), axis=1)]
  transfers between devices with their start and end apart: 18 -> 26, of which waited for: 8 -> 10; matrix products, arithmetic and copies ran while one was open for 11% -> 15% of each run, Pallas kernels for 22% -> 32%
where the time goes in v2:
time: 353 us; the launch traced here: 346 us
  Pallas kernels  111 us (31%)
  blocking collectives  61.8 us (18%)
  waiting for transfers between devices  45 us (13%)
  starting transfers between devices  42.5 us (12%)
  other arithmetic  30.3 us (9%)
  local copies, waits for them, and re-layouts  30.1 us (9%)
  between operations  15.2 us (4%)
  matrix products  9.54 us (3%)
    pallas_call x1, Pallas kernels, local_heads(): pl.pallas_call(partial(attend_back_kernel, 1), grid=(shards,), in_specs=b...  24.3 us
    ppermute x10, waiting for transfers between devices, hop(): return lax.ppermute(value, 'shard', [(i, i ^ step) for i in range(8)])  23.2 us
    pallas_call x1, Pallas kernels, local_heads(): pl.pallas_call(partial(attend_back_kernel, 0), grid=(shards,), in_specs=b...  22.2 us
    all_gather x1, blocking collectives, local_heads(): small = lax.all_gather(small, 'shard', axis=0).astype(f32)  17.9 us
    pallas_call x1, Pallas kernels, local_heads(): pl.pallas_call(attend_kernel, grid=(shards,), in_specs=[two_heads, whole(...  17.8 us
    all_gather x1, blocking collectives, local_heads(): high = lax.all_gather(after(mod_own, w_cols), 'grp', axis=1, tiled=True)  16.8 us
    unnamed x106, local copies, waits for them, and re-layouts  16.2 us
    pallas_call x1, Pallas kernels, local_heads(): pl.pallas_call(qkv_kernel, grid_spec=pltpu.PrefetchScalarGridSpec(num_sca...  16 us
  transfers between devices with their start and end apart: 26, of which 10 were waited for; matrix products, arithmetic and copies ran while one was open for 15% of the time, Pallas kernels for 32%

profile of v2, /device:TPU:0, one launch (start us, length us, event | category | flops | bytes accessed | tf_op | source)
XLA Modules:
  0.0 345.7 jit_solution(9993444099530116692)
XLA Ops:
  13.1 7.3 %all-to-all-start = ((bf16[32,128,128]{2,1,0:T(8,128)(2,1)}), bf16[32,128,128]{2,1,0:T(8,128)(2,1)S(1)}, u32[]{:S(2)}, u32[]{:S(2)}) async-start(bf16[32,128,128]{2,1,0:T(8,128)(2,1)} %bitcast.8), calls=%async_computation | async-start | bytes 2097152 | tf_op jit(solution)/shard_map/all_to_all | solution.py:814
  21.7 17.9 %all_gather.25 = bf16[8,34,1536]{2,1,0:T(8,128)(2,1)S(1)} all-gather(bf16[1,34,1536]{2,1,0:T(8,128)(2,1)S(1)} %pad_maximum_fusion.9), channel_id=1, replica_groups=mesh['grp'=4,'shard'=8] {'shard'}, dimensions={0}, use_global_device_ids=true | all-gather | bytes 940032 | tf_op jit(solution)/shard_map/all_gather | solution.py:816
  50.1 6.9 %all-to-all-done = bf16[32,128,128]{2,1,0:T(8,128)(2,1)S(1)} async-done(((bf16[32,128,128]{2,1,0:T(8,128)(2,1)}), bf16[32,128,128]{2,1,0:T(8,128)(2,1)S(1)}, u32[]{:S(2)}, u32[]{:S(2)}) %all-to-all-start) | async-done | bytes 1048608 | tf_op jit(solution)/shard_map/all_to_all | solution.py:814
  57.9 16.8 %all_gather.26.refs_1_ = bf16[32,6144]{1,0:T(8,128)(2,1)} all-gather(bf16[32,1536]{1,0:T(8,128)(2,1)} %after.17), channel_id=1, replica_groups=mesh['grp'=4,'shard'=8] {'grp'}, dimensions={1}, use_global_device_ids=true | all-gather | bytes 491520 | tf_op jit(solution)/shard_map/all_gather | solution.py:821
  75.2 4.7 %collective-permute-done.refs_0_ = bf16[256,1024]{1,0:T(8,128)(2,1)} collective-permute-done((bf16[256,1024]{1,0:T(8,128)(2,1)}, bf16[256,1024]{1,0:T(8,128)(2,1)}, u32[]{:S(2)}, u32[]{:S(2)}) %collective-permute-start) | collective-permute-done | bytes 524320 | tf_op jit(solution)/shard_map/ppermute | solution.py:753
  87.3 16.0 %qkv.1 = (bf16[2,2048,128]{2,1,0:T(8,128)(2,1)}, bf16[2,2048,128]{2,1,0:T(8,128)(2,1)}, bf16[2,2048,128]{2,1,0:T(8,128)(2,1)}, bf16[2048,1024]{1,0:T(8,128)(2,1)}) custom-call(s32[8]{0:T(128)} %broadcast_xor_fusion.order_ref, s32[8,9]{1,0:T(8,128)} %fusion.20.seg_ref, bf16[1,256,1024]{2,1,0:T(8,128)(2,1)} %bitcast.136, ...), custom_call_target="tpu_custom_call" | custom-call | flops 1048576 | bytes 65536 | tf_op jit(solution)/shard_map/qkv/pallas_call | solution.py:849
  103.3 17.8 %attend.1 = (bf16[2048,128]{1,0:T(8,128)(2,1)}, f32[2048,128]{1,0:T(8,128)}, f32[2048,128]{1,0:T(8,128)}) custom-call(bf16[2,2048,128]{2,1,0:T(8,128)(2,1)} %get-tuple-element.41.q_ref, bf16[2,2048,128]{2,1,0:T(8,128)(2,1)} %get-tuple-element.42.k_ref, bf16[2,2048,128]{2,1,0:T(8,128)(2,1)} %get-tuple-element.43.v_ref), custom_call_target="tpu_custom_call" | custom-call | flops 1048576 | bytes 65536 | tf_op jit(solution)/shard_map/attend/pallas_call | solution.py:867
  121.1 14.2 %all_to_all.30.o_ref.refs_1_ = bf16[8,256,128]{2,1,0:T(8,128)(2,1)} all-to-all(bf16[8,256,128]{2,1,0:T(8,128)(2,1)} %bitcast.149), channel_id=1, replica_groups=mesh['grp'=4,'shard'=8] {'shard'}, dimensions={0} | all-to-all | bytes 1048576 | tf_op jit(solution)/shard_map/all_to_all | solution.py:878
  136.6 14.6 %block.1 = (bf16[256,1024]{1,0:T(8,128)(2,1)}, f32[256,1024]{1,0:T(8,128)}, bf16[8,256,128]{2,1,0:T(8,128)(2,1)}, bf16[256,4096]{1,0:T(8,128)(2,1)}, bf16[256,20...) custom-call(s32[8]{0:T(128)} %broadcast_xor_fusion.order_ref, ...), custom_call_target="tpu_custom_call" | custom-call | flops 1048576 | bytes 65536 | tf_op jit(solution)/shard_map/block/pallas_call | solution.py:881
  151.7 3.5 %all-to-all-start.2 = ((bf16[8,256,128]{2,1,0:T(8,128)(2,1)}), bf16[8,256,128]{2,1,0:T(8,128)(2,1)S(1)}, u32[]{:S(2)}, u32[]{:S(2)}) async-start(bf16[8,256,128]{2,1,0:T(8,128)(2,1)} %get-tuple-element.46), calls=%async_computation.2 | async-start | bytes 1048576 | tf_op jit(solution)/shard_map/all_to_all | solution.py:902
  158.4 11.2 %weight_grads.1 = (bf16[2,2,640,256]{3,2,1,0:T(8,128)(2,1)}, bf16[2,2,640,256]{3,2,1,0:T(8,128)(2,1)}, bf16[2,2,640,256]{3,2,1,0:T(8,128)(2,1)}, bf16[2,2,640,256]{3,2,1,0:T(8,128)(2,1)}) custom-call(s32[8]{0:T(128)} %broadcast_xor_fusion.order_ref, s32[1]{0:T(128)} %bitcast.23.group_ref, bf16[256,2048]{1,0:T(8,128)(2,1)} %get-tuple-element.47.keep_ref, ...), custom_call_target="tpu_custom_call" | custom-call | flops 1048576 | bytes 65536 | tf_op jit(solution)/shard_map/weight_grads/pallas_call | solution.py:906
  171.0 22.2 %attend_back_first.1 = (bf16[2048,128]{1,0:T(8,128)(2,1)}, bf16[2048,128]{1,0:T(8,128)(2,1)}) custom-call(bf16[2,2048,128]{2,1,0:T(8,128)(2,1)} %get-tuple-element.41.q_ref, bf16[2,2048,128]{2,1,0:T(8,128)(2,1)} %get-tuple-element.42.k_ref, bf16[2,2048,128]{2,1,0:T(8,128)(2,1)} %get-tuple-element.43.v_ref, bf16[2048,128]{1,0:T(8,128)(2,1)} %after.23.do_ref, ...), custom_call_target="tpu_custom_call" | custom-call | flops 1048576 | bytes 65536 | tf_op jit(solution)/shard_map/attend_back_first/pallas_call | solution.py:928
  193.3 15.7 %collective-permute-done.7.refs_0_ = bf16[2,2,640,256]{3,2,1,0:T(8,128)(2,1)S(1)} collective-permute-done((bf16[2,2,640,256]{3,2,1,0:T(8,128)(2,1)}, bf16[2,2,640,256]{3,2,1,0:T(8,128)(2,1)S(1)}, u32[]{:S(2)}, u32[]{:S(2)}) %collective-permute-start.7) | collective-permute-done | bytes 1310752 | tf_op jit(solution)/shard_map/ppermute | solution.py:753
  215.1 3.7 %all-to-all-start.3 = ((bf16[8,256,128]{2,1,0:T(8,128)(2,1)}), bf16[8,256,128]{2,1,0:T(8,128)(2,1)S(1)}, u32[]{:S(2)}, u32[]{:S(2)}) async-start(bf16[8,256,128]{2,1,0:T(8,128)(2,1)} %bitcast.24), calls=%async_computation.3 | async-start | bytes 1048576 | tf_op jit(solution)/shard_map/all_to_all | solution.py:943
  224.6 24.3 %attend_back_second.1 = (bf16[2048,128]{1,0:T(8,128)(2,1)}, bf16[2048,384]{1,0:T(8,128)(2,1)}, f32[3,128]{1,0:T(4,128)}) custom-call(bf16[2,2048,128]{2,1,0:T(8,128)(2,1)} %get-tuple-element.41.q_ref, bf16[2,2048,128]{2,1,0:T(8,128)(2,1)} %get-tuple-element.42.k_ref, bf16[2,2048,128]{2,1,0:T(8,128)(2,1)} %get-tuple-element.43.v_ref, ...), custom_call_target="tpu_custom_call" | custom-call | flops 1048576 | bytes 65536 | tf_op jit(solution)/shard_map/attend_back_second/pallas_call | solution.py:944
  255.6 3.2 collective-permute-start.10
  261.9 3.6 %all-to-all-start.4 = ((bf16[8,256,256]{2,1,0:T(8,128)(2,1)}), bf16[8,256,256]{2,1,0:T(8,128)(2,1)S(1)}, u32[]{:S(2)}, u32[]{:S(2)}) async-start(bf16[8,256,256]{2,1,0:T(8,128)(2,1)} %pad_maximum_fusion.1), calls=%async_computation.4 | async-start | bytes 2097152 | tf_op jit(solution)/shard_map/all_to_all | solution.py:964
  266.3 5.0 %convolution_convert_fusion.1 = bf16[1024,384]{1,0:T(8,128)(2,1)S(1)} fusion(bf16[2048,1024]{1,0:T(8,128)(2,1)} %get-tuple-element.68, bf16[2048,384]{1,0:T(8,128)(2,1)} %after.31), kind=kOutput, calls=%fused_computation.6 | convolution fusion | flops 1611005952 | bytes 6553600 | tf_op jit(solution)/shard_map/dot_general | solution.py:380
  272.7 8.1 %all-to-all-done.4.second_ref = bf16[8,256,256]{2,1,0:T(8,128)(2,1)S(1)} async-done(((bf16[8,256,256]{2,1,0:T(8,128)(2,1)}), bf16[8,256,256]{2,1,0:T(8,128)(2,1)S(1)}, u32[]{:S(2)}, u32[]{:S(2)}) %all-to-all-start.4) | async-done | bytes 1048608 | tf_op jit(solution)/shard_map/all_to_all | solution.py:964
  280.8 3.6 %all-to-all-start.5 = ((bf16[32,128,128]{2,1,0:T(8,128)(2,1)}), bf16[32,128,128]{2,1,0:T(8,128)(2,1)}, u32[]{:S(2)}, u32[]{:S(2)}) async-start(bf16[32,128,128]{2,1,0:T(8,128)(2,1)} %bitcast.141), calls=%async_computation.5 | async-start | bytes 2097152 | tf_op jit(solution)/shard_map/all_to_all | solution.py:981
  288.5 5.0 %input_grad.1 = (f32[256,1024]{1,0:T(8,128)}, f32[8,1024]{1,0:T(8,128)S(1)}) custom-call(s32[1]{0:T(128)} %bitcast.21.base_ref, s32[8,9]{1,0:T(8,128)S(1)} %copy-done.6, bf16[8,256,128]{2,1,0:T(8,128)(2,1)S(1)} %all-to-all-done.3.first_ref, bf16[8,256,256]{2,1,0:T(8,128)(2,1)S(1)} %all-to-all-done.4.second_ref, bf16[8,1024,384]{2,1,0:T(8,128)(2,1)S(1)} %bitcast.130, ...), custom_call_target="tpu_custom_call" | custom-call | flops 1048576 | bytes 65536 | tf_op jit(solution)/shard_map/input_grad/pallas_call | solution.py:966
  296.5 12.9 %all-gather.3 = f32[8,4,6144]{2,1,0:T(4,128)S(1)} all-gather(f32[1,4,6144]{2,1,0:T(4,128)} %bitcast.145), channel_id=4, replica_groups=mesh['grp'=4,'shard'=8] {'shard'}, dimensions={0}, use_global_device_ids=true | all-gather | bytes 884736 | tf_op jit(solution)/shard_map/all_gather | solution.py:991
  311.7 4.4 %collective-permute-start.13 = (f32[9,1536]{1,0:T(8,128)S(1)}, f32[9,1536]{1,0:T(8,128)S(1)}, u32[]{:S(2)}, u32[]{:S(2)}) collective-permute-start(f32[9,1536]{1,0:T(8,128)S(1)} %get-tuple-element.103), channel_id=1, source_target_pairs={{0,24},{8,0},{16,8},{24,16},{1,25},{9,1},{17,9},{25,17},{2,26},{10... | collective-permute-start | bytes 165896 | tf_op jit(solution)/shard_map/ppermute | solution.py:735
  319.3 6.4 %collective-permute-done.14 = f32[9,1536]{1,0:T(8,128)S(1)} collective-permute-done((f32[9,1536]{1,0:T(8,128)S(1)}, f32[9,1536]{1,0:T(8,128)S(1)}, u32[]{:S(2)}, u32[]{:S(2)}) %collective-permute-start.14) | collective-permute-done | bytes 55328 | tf_op jit(solution)/shard_map/ppermute | solution.py:735
  (259 shorter events, 81.7 us)
Async XLA Ops:
  7.2 129.4 %all-gather.7.cloned.1.call-start = ((), (), s32[]{:S(2)}) async-start(), calls=%async_computation.6 | async-start | bytes 10813440 | tf_op jit(solution)/shard_map/all_gather | solution.py:831
  13.1 43.8 %all-to-all-start = ((bf16[32,128,128]{2,1,0:T(8,128)(2,1)}), bf16[32,128,128]{2,1,0:T(8,128)(2,1)S(1)}, u32[]{:S(2)}, u32[]{:S(2)}) async-start(bf16[32,128,128]{2,1,0:T(8,128)(2,1)} %bitcast.8), calls=%async_computation | async-start | bytes 2097152 | tf_op jit(solution)/shard_map/all_to_all | solution.py:814
  20.4 264.0 %all-gather.9.cloned.1.call-start = ((), (), s32[]{:S(2)}) async-start(), calls=%async_computation.7 | async-start | bytes 7077888 | tf_op jit(solution)/shard_map/all_gather | solution.py:965
  42.0 32.6 %collective-permute-start.2 = (bf16[256,1024]{1,0:T(8,128)(2,1)}, bf16[256,1024]{1,0:T(8,128)(2,1)}, u32[]{:S(2)}, u32[]{:S(2)}) collective-permute-start(bf16[256,1024]{1,0:T(8,128)(2,1)} %after.16), channel_id=1, source_target_pairs={{0,6},{1,7},{2,4},{3,5},{4,2},{5,3},{6,0},{7,1},{8,14},{9,15},{10,... | collective-permute-start | bytes 1572872 | tf_op jit(solution)/shard_map/ppermute | solution.py:753
  44.1 31.1 %collective-permute-start.1 = (bf16[256,1024]{1,0:T(8,128)(2,1)}, bf16[256,1024]{1,0:T(8,128)(2,1)}, u32[]{:S(2)}, u32[]{:S(2)}) collective-permute-start(bf16[256,1024]{1,0:T(8,128)(2,1)} %after.16), channel_id=1, source_target_pairs={{0,4},{1,5},{2,6},{3,7},{4,0},{5,1},{6,2},{7,3},{8,12},{9,13},{10,... | collective-permute-start | bytes 1572872 | tf_op jit(solution)/shard_map/ppermute | solution.py:753
  44.5 35.4 %collective-permute-start = (bf16[256,1024]{1,0:T(8,128)(2,1)}, bf16[256,1024]{1,0:T(8,128)(2,1)}, u32[]{:S(2)}, u32[]{:S(2)}) collective-permute-start(bf16[256,1024]{1,0:T(8,128)(2,1)} %after.16), channel_id=1, source_target_pairs={{0,2},{1,3},{2,0},{3,1},{4,6},{5,7},{6,4},{7,5},{8,10},{9,11},{10,... | collective-permute-start | bytes 1572872 | tf_op jit(solution)/shard_map/ppermute | solution.py:753
  151.2 5.9 %collective-permute-start.5 = (bf16[256,4096]{1,0:T(8,128)(2,1)}, bf16[256,4096]{1,0:T(8,128)(2,1)S(1)}, u32[]{:S(2)}, u32[]{:S(2)}) collective-permute-start(bf16[256,4096]{1,0:T(8,128)(2,1)} %get-tuple-element.49.pair_ref), channel_id=1, source_target_pairs={{0,1},{1,0},{2,3},{3,2},{4,5},{5,4},{6,7},{7,6},{8,9},{9,8},{10,11... | collective-permute-start | bytes 6291464 | tf_op jit(solution)/shard_map/ppermute | solution.py:753
  151.7 17.9 %all-to-all-start.2 = ((bf16[8,256,128]{2,1,0:T(8,128)(2,1)}), bf16[8,256,128]{2,1,0:T(8,128)(2,1)S(1)}, u32[]{:S(2)}, u32[]{:S(2)}) async-start(bf16[8,256,128]{2,1,0:T(8,128)(2,1)} %get-tuple-element.46), calls=%async_computation.2 | async-start | bytes 1048576 | tf_op jit(solution)/shard_map/all_to_all | solution.py:902
  170.4 38.5 %collective-permute-start.7 = (bf16[2,2,640,256]{3,2,1,0:T(8,128)(2,1)}, bf16[2,2,640,256]{3,2,1,0:T(8,128)(2,1)S(1)}, u32[]{:S(2)}, u32[]{:S(2)}) collective-permute-start(bf16[2,2,640,256]{3,2,1,0:T(8,128)(2,1)} %after.22.refs_2_), channel_id=1, source_target_pairs={{0,4},{1,5},{2,6},{3,7},{4,0},{5,1},{6,2},{7,3},{8,12},{9,13},{10,... | collective-permute-start | bytes 3932168 | tf_op jit(solution)/shard_map/ppermute | solution.py:753
  170.4 48.3 %collective-permute-start.6 = (bf16[2,2,640,256]{3,2,1,0:T(8,128)(2,1)}, bf16[2,2,640,256]{3,2,1,0:T(8,128)(2,1)S(1)}, u32[]{:S(2)}, u32[]{:S(2)}) collective-permute-start(bf16[2,2,640,256]{3,2,1,0:T(8,128)(2,1)} %after.21.refs_1_), channel_id=1, source_target_pairs={{0,2},{1,3},{2,0},{3,1},{4,6},{5,7},{6,4},{7,5},{8,10},{9,11},{10,... | collective-permute-start | bytes 3932168 | tf_op jit(solution)/shard_map/ppermute | solution.py:753
  212.4 40.6 %collective-permute-start.9 = (bf16[2,640,256]{2,1,0:T(8,128)(2,1)}, bf16[2,640,256]{2,1,0:T(8,128)(2,1)}, u32[]{:S(2)}, u32[]{:S(2)}) collective-permute-start(bf16[2,640,256]{2,1,0:T(8,128)(2,1)} %fusion.4.refs_2_), channel_id=1, source_target_pairs={{0,2},{1,3},{2,0},{3,1},{4,6},{5,7},{6,4},{7,5},{8,10},{9,11},{10,... | collective-permute-start | bytes 1966088 | tf_op jit(solution)/shard_map/ppermute | solution.py:753
  215.1 46.8 %all-to-all-start.3 = ((bf16[8,256,128]{2,1,0:T(8,128)(2,1)}), bf16[8,256,128]{2,1,0:T(8,128)(2,1)S(1)}, u32[]{:S(2)}, u32[]{:S(2)}) async-start(bf16[8,256,128]{2,1,0:T(8,128)(2,1)} %bitcast.24), calls=%async_computation.3 | async-start | bytes 1048576 | tf_op jit(solution)/shard_map/all_to_all | solution.py:943
  222.7 36.6 %collective-permute-start.8 = (bf16[2,640,256]{2,1,0:T(8,128)(2,1)}, bf16[2,640,256]{2,1,0:T(8,128)(2,1)S(1)}, u32[]{:S(2)}, u32[]{:S(2)}) collective-permute-start(bf16[2,640,256]{2,1,0:T(8,128)(2,1)} %fusion.3.refs_1_), channel_id=1, source_target_pairs={{0,4},{1,5},{2,6},{3,7},{4,0},{5,1},{6,2},{7,3},{8,12},{9,13},{10,... | collective-permute-start | bytes 1966088 | tf_op jit(solution)/shard_map/ppermute | solution.py:753
  255.6 38.7 %collective-permute-start.10 = (bf16[640,256]{1,0:T(8,128)(2,1)}, bf16[640,256]{1,0:T(8,128)(2,1)}, u32[]{:S(2)}, u32[]{:S(2)}) collective-permute-start(bf16[640,256]{1,0:T(8,128)(2,1)} %get-tuple-element.89), channel_id=1, source_target_pairs={{0,24},{8,0},{16,8},{24,16},{1,25},{9,1},{17,9},{25,17},{2,26},{10... | collective-permute-start | bytes 983048 | tf_op jit(solution)/shard_map/ppermute | solution.py:735
  258.8 35.5 %collective-permute-start.11 = (bf16[640,256]{1,0:T(8,128)(2,1)}, bf16[640,256]{1,0:T(8,128)(2,1)}, u32[]{:S(2)}, u32[]{:S(2)}) collective-permute-start(bf16[640,256]{1,0:T(8,128)(2,1)} %get-tuple-element.90), channel_id=1, source_target_pairs={{0,16},{8,24},{16,0},{24,8},{1,17},{9,25},{17,1},{25,9},{2,18},{10... | collective-permute-start | bytes 983048 | tf_op jit(solution)/shard_map/ppermute | solution.py:735
  261.9 18.9 %all-to-all-start.4 = ((bf16[8,256,256]{2,1,0:T(8,128)(2,1)}), bf16[8,256,256]{2,1,0:T(8,128)(2,1)S(1)}, u32[]{:S(2)}, u32[]{:S(2)}) async-start(bf16[8,256,256]{2,1,0:T(8,128)(2,1)} %pad_maximum_fusion.1), calls=%async_computation.4 | async-start | bytes 2097152 | tf_op jit(solution)/shard_map/all_to_all | solution.py:964
  266.2 28.1 %collective-permute-start.12 = (bf16[640,256]{1,0:T(8,128)(2,1)}, bf16[640,256]{1,0:T(8,128)(2,1)}, u32[]{:S(2)}, u32[]{:S(2)}) collective-permute-start(bf16[640,256]{1,0:T(8,128)(2,1)} %slice_bitcast_fusion), channel_id=1, source_target_pairs={{0,8},{8,16},{16,24},{24,0},{1,9},{9,17},{17,25},{25,1},{2,10},{10... | collective-permute-start | bytes 983048 | tf_op jit(solution)/shard_map/ppermute | solution.py:735
  280.8 55.5 %all-to-all-start.5 = ((bf16[32,128,128]{2,1,0:T(8,128)(2,1)}), bf16[32,128,128]{2,1,0:T(8,128)(2,1)}, u32[]{:S(2)}, u32[]{:S(2)}) async-start(bf16[32,128,128]{2,1,0:T(8,128)(2,1)} %bitcast.141), calls=%async_computation.5 | async-start | bytes 2097152 | tf_op jit(solution)/shard_map/all_to_all | solution.py:981
  311.7 7.6 %collective-permute-start.13 = (f32[9,1536]{1,0:T(8,128)S(1)}, f32[9,1536]{1,0:T(8,128)S(1)}, u32[]{:S(2)}, u32[]{:S(2)}) collective-permute-start(f32[9,1536]{1,0:T(8,128)S(1)} %get-tuple-element.103), channel_id=1, source_target_pairs={{0,24},{8,0},{16,8},{24,16},{1,25},{9,1},{17,9},{25,17},{2,26},{10... | collective-permute-start | bytes 165896 | tf_op jit(solution)/shard_map/ppermute | solution.py:735
  316.1 9.6 %collective-permute-start.14 = (f32[9,1536]{1,0:T(8,128)S(1)}, f32[9,1536]{1,0:T(8,128)S(1)}, u32[]{:S(2)}, u32[]{:S(2)}) collective-permute-start(f32[9,1536]{1,0:T(8,128)S(1)} %get-tuple-element.104), channel_id=1, source_target_pairs={{0,16},{8,24},{16,0},{24,8},{1,17},{9,25},{17,1},{25,9},{2,18},{10... | collective-permute-start | bytes 165896 | tf_op jit(solution)/shard_map/ppermute | solution.py:735
  316.1 9.6 %collective-permute-start.15 = (f32[9,1536]{1,0:T(8,128)S(1)}, f32[9,1536]{1,0:T(8,128)S(1)}, u32[]{:S(2)}, u32[]{:S(2)}) collective-permute-start(f32[9,1536]{1,0:T(8,128)S(1)} %get-tuple-element.105), channel_id=1, source_target_pairs={{0,8},{8,16},{16,24},{24,0},{1,9},{9,17},{17,25},{25,1},{2,10},{10... | collective-permute-start | bytes 165896 | tf_op jit(solution)/shard_map/ppermute | solution.py:735
  327.4 8.3 %collective-permute-start.16 = (f32[32,128]{1,0:T(8,128)S(1)}, f32[32,128]{1,0:T(8,128)S(1)}, u32[]{:S(2)}, u32[]{:S(2)}) collective-permute-start(f32[32,128]{1,0:T(8,128)S(1)} %fusion.18), channel_id=1, source_target_pairs={{0,24},{8,0},{16,8},{24,16},{1,25},{9,1},{17,9},{25,17},{2,26},{10... | collective-permute-start | bytes 49160 | tf_op jit(solution)/shard_map/ppermute | solution.py:729
  328.7 7.0 %collective-permute-start.17 = (f32[32,128]{1,0:T(8,128)S(1)}, f32[32,128]{1,0:T(8,128)S(1)}, u32[]{:S(2)}, u32[]{:S(2)}) collective-permute-start(f32[32,128]{1,0:T(8,128)S(1)} %fusion.18), channel_id=1, source_target_pairs={{0,16},{8,24},{16,0},{24,8},{1,17},{9,25},{17,1},{25,9},{2,18},{10... | collective-permute-start | bytes 49160 | tf_op jit(solution)/shard_map/ppermute | solution.py:729
  329.4 6.3 %collective-permute-start.18 = (f32[32,128]{1,0:T(8,128)S(1)}, f32[32,128]{1,0:T(8,128)S(1)}, u32[]{:S(2)}, u32[]{:S(2)}) collective-permute-start(f32[32,128]{1,0:T(8,128)S(1)} %fusion.18), channel_id=1, source_target_pairs={{0,8},{8,16},{16,24},{24,0},{1,9},{9,17},{17,25},{25,1},{2,10},{10... | collective-permute-start | bytes 49160 | tf_op jit(solution)/shard_map/ppermute | solution.py:729
  (44 other events, 205.4 us)
Sparse Core Ops, SparseCore 0:
  11.4 108.0 all-gather.6
  135.5 54.4 all-gather.8
